TPU v7x, 32 devices: a whole 2x2x4 slice. The times are simulated.
32 devices in a mesh: row: 4 (over y, x), col: 8 (over z, core).
Axes of the slice: x: 2, y: 2, z: 4, core: 2. Of those that a mesh axis runs over, the one named last changes fastest.
Arguments:
- start_block: float32 [96, 256, 1024], P(None, 'row', 'col'), may hold values from -6 to 6
- stiffness: float32 [256, 1024], P('row', 'col'), may hold values from 0.5 to 2
Outputs:
- basis: float32 [96, 256, 1024], P(None, 'row', 'col')
- projected: float32 [96, 96], replicated
All inputs are finite; a program needn't handle non-finite values.
Results may differ from a plain program's by a relative error of at most 0.000086.
Values sent between devices are 32-bit elements; how exact they have to be, the bound alone decides.
No kernel may reach another device: no remote copies, remote signals or barrier semaphores. Data moves between devices by JAX's collectives and lax.ppermute only.
A program may use at most 64 MiB of HBM per device.

v0:
```python
import functools
import jax
import jax.numpy as jnp
from jax import lax
from jax.experimental import pallas as pl
from jax.experimental.pallas import tpu as pltpu
from jax.sharding import PartitionSpec as P

DEGREE = 4
TOP = 129.0
CUT = 16.0
SHIFT = 1.0
CENTER = (TOP + CUT) / 2.0
HALF = (TOP - CUT) / 2.0
LEAD = (CENTER - SHIFT) / HALF
HALO = 2 * DEGREE + 1
MARGIN = HALO - 1
LANES = 128
PAD = 16
GROUP = 4
F32 = jnp.float32
BF16 = jnp.bfloat16
MIB = 2**20
VMEM = pl.BlockSpec(memory_space=pltpu.VMEM)
HBM = pl.BlockSpec(memory_space=pl.ANY)


def split(values):
    high = values.astype(BF16)
    low = (values - high.astype(F32)).astype(BF16)
    return high, low


def even(index):
    return lax.rem(index, 2) == 0


def loop(count, work):
    def one(i, carry):
        work(i)
        return carry

    lax.fori_loop(0, count, one, 0)


def params(limit):
    return pltpu.CompilerParams(vmem_limit_bytes=limit * MIB)


def padded(rows, cols):
    return jax.ShapeDtypeStruct((rows + 2 * HALO, cols + 2 * PAD, LANES), F32)


def lanes_up(block, stiff):
    vectors, cols = block.shape
    fill = jnp.zeros((LANES - vectors - 8, cols), F32)
    return jnp.concatenate([block, jnp.broadcast_to(stiff, (8, cols)), fill], axis=0).T


def spread_stiffness(row):
    return jnp.broadcast_to(row * (2.0 / HALF), (LANES, row.shape[1])).T


def turn_kernel(block_ref, stiff_ref, field, near, far, one, two, held, sems):
    chunks, vectors, step, cols = held.shape
    rows = chunks * step
    col_first, row_first = even(lax.axis_index("col")), even(lax.axis_index("row"))
    copies = [
        pltpu.make_async_copy(block_ref.at[:, pl.ds(i * step, step), :], held.at[i], sems.at[i])
        for i in range(chunks)
    ]
    for copy in copies:
        copy.start()

    def chunk(i):
        pltpu.make_async_copy(block_ref.at[:, pl.ds(i * step, step), :], held.at[i], sems.at[i]).wait()
        for r in range(step):
            x = i * step + r
            turned = lanes_up(held[i, :, r, :], stiff_ref[pl.ds(x, 1), :])
            field[HALO + x, PAD : PAD + cols, :] = turned
            head, tail = turned[:HALO], turned[cols - HALO :]
            near[pl.ds(x * HALO, HALO), :] = jnp.where(col_first, tail, head)
            far[pl.ds(x * HALO, HALO), :] = jnp.where(col_first, head, tail)

    loop(chunks, chunk)
    for r in range(HALO):
        end = rows - HALO + r
        head = held[r // step, :, r % step, :]
        tail = held[end // step, :, end % step, :]
        one[r * vectors : (r + 1) * vectors, :] = jnp.where(row_first, tail, head)
        two[r * vectors : (r + 1) * vectors, :] = jnp.where(row_first, head, tail)


def turn(block, stiffness):
    vectors, rows, cols = block.shape
    side = jax.ShapeDtypeStruct((rows * HALO, LANES), F32)
    end = jax.ShapeDtypeStruct((HALO * vectors, cols), F32)
    step = 8
    return pl.pallas_call(
        turn_kernel,
        in_specs=[HBM, VMEM],
        out_specs=[VMEM] * 5,
        out_shape=[padded(rows, cols), side, side, end, end],
        scratch_shapes=[
            pltpu.VMEM((rows // step, vectors, step, cols), F32),
            pltpu.SemaphoreType.DMA((rows // step,)),
        ],
        compiler_params=params(24),
        cost_estimate=pl.CostEstimate(flops=0, bytes_accessed=4 * vectors * rows * cols * 2, transcendentals=0),
    )(block, stiffness)


def stiff_kernel(stiff_ref, field, stiff):
    rows, cols = stiff_ref.shape
    step = 8

    def some(i):
        for r in range(step):
            x = i * step + r
            stiff[HALO + x, PAD : PAD + cols, :] = spread_stiffness(stiff_ref[pl.ds(x, 1), :])

    loop(rows // step, some)


def own_stiffness(stiffness, field):
    rows, cols = stiffness.shape
    return pl.pallas_call(
        stiff_kernel,
        in_specs=[VMEM, HBM],
        out_specs=VMEM,
        out_shape=padded(rows, cols),
        compiler_params=params(16),
        cost_estimate=pl.CostEstimate(flops=0, bytes_accessed=4 * LANES * rows * cols, transcendentals=0),
    )(stiffness, field)


def corner_kernel(vectors, field_in, stiff_in, stiff_ref, near, far, field, stiff, one, two):
    rows, cols = stiff_ref.shape
    col_first, row_first = even(lax.axis_index("col")), even(lax.axis_index("row"))
    step = 8
    ends = (PAD - MARGIN, PAD + cols)

    def some(i):
        for r in range(step):
            x = i * step + r
            a, b = near[pl.ds(x * HALO, HALO), :], far[pl.ds(x * HALO, HALO), :]
            field[HALO + x, PAD - HALO : PAD, :] = jnp.where(col_first, b, a)
            field[HALO + x, PAD + cols : PAD + cols + HALO, :] = jnp.where(col_first, a, b)
        for r in range(step):
            x = HALO + i * step + r
            for y in ends:
                lane = field[x, y : y + MARGIN, vectors : vectors + 1] * (2.0 / HALF)
                stiff[x, y : y + MARGIN, :] = jnp.broadcast_to(lane, (MARGIN, LANES))

    loop(rows // step, some)
    last = rows - HALO
    for out, start in ((one, jnp.where(row_first, last, 0)), (two, jnp.where(row_first, 0, last))):
        for r in range(HALO):
            for e, y in enumerate(ends):
                out[(2 * r + e) * MARGIN : (2 * r + e + 1) * MARGIN, :] = field[HALO + start + r, y : y + MARGIN, :]
        base = 2 * HALO * MARGIN
        out[base:, :] = jnp.zeros((out.shape[0] - base, LANES), F32)
    base = 2 * HALO * MARGIN
    head, tail = stiff_ref[:HALO, :], stiff_ref[last:, :]
    one[base : base + HALO, :] = jnp.where(row_first, tail, head)
    two[base : base + HALO, :] = jnp.where(row_first, head, tail)


def corners(vectors, field, stiff, stiffness, near, far):
    rows, cols = stiffness.shape
    corner = jax.ShapeDtypeStruct((2 * HALO * MARGIN + 16, LANES), F32)
    return pl.pallas_call(
        functools.partial(corner_kernel, vectors),
        in_specs=[VMEM] * 5,
        out_specs=[VMEM] * 4,
        out_shape=[padded(rows, cols), padded(rows, cols), corner, corner],
        input_output_aliases={0: 0, 1: 1},
        compiler_params=params(16),
    )(field, stiff, stiffness, near, far)


def around(ref, x, y, step):
    mid = ref[pl.ds(x - 1, step + 2), pl.ds(y, 8), :]
    left = ref[pl.ds(x, step), pl.ds(y - 1, 8), :]
    right = ref[pl.ds(x, step), pl.ds(y + 1, 8), :]
    return ((mid[:-2] + mid[2:]) + (left + right)) - 4.0 * mid[1:-1]


def bend(field, stiff, inner, x, y, step):
    at = (pl.ds(x, step), pl.ds(y, 8))
    inner[*at, :] = stiff[*at, :] * around(field, x, y, step)


def advance(k, current, inner, following, x, y, step):
    at = (pl.ds(x, step), pl.ds(y, 8))
    image = around(inner, x, y, step)
    here = current[*at, :]
    if k == 0:
        following[*at, :] = LEAD * here - 0.5 * image
    else:
        following[*at, :] = (2.0 * LEAD * here - following[*at, :]) - image


def root_bend(field, stiff, inner, x, y, step):
    at = (pl.ds(x, step), pl.ds(y, 8))
    weight = stiff[*at, :]
    inner[*at, :] = weight * lax.rsqrt(weight) * around(field, x, y, step)


def sweep(low, high, ys, work):
    step = 4
    whole = (high - low) // step

    def chunk(i):
        for y in ys:
            work(low + i * step, y, step)

    loop(whole, chunk)
    rest = (high - low) - whole * step
    if rest:
        for y in ys:
            work(high - rest, y, rest)


def clear_cols(field, low, high, cols):
    col, count = lax.axis_index("col"), lax.axis_size("col")

    def at(start):
        field[low:high, start : start + MARGIN, :] = jnp.zeros((high - low, MARGIN, LANES), F32)

    pl.when(col == 0)(lambda: at(PAD - MARGIN))
    pl.when(col == count - 1)(lambda: at(PAD + cols))


def clear_rows(field, rows, cols):
    row, count = lax.axis_index("row"), lax.axis_size("row")

    def at(start):
        wide = cols + 2 * MARGIN
        for x in range(start, start + HALO):
            field[x, PAD - MARGIN : PAD + cols + MARGIN, :] = jnp.zeros((wide, LANES), F32)

    pl.when(row == 0)(lambda: at(0))
    pl.when(row == count - 1)(lambda: at(HALO + rows))


def prepare(slot, x, j, vectors, cols, field, inner, turned, lhs):
    cells = field[HALO + x, PAD : PAD + cols, :].T[:vectors]
    turned[x] = cells
    lhs[slot, 0, :, j * cols : (j + 1) * cols] = cells.astype(BF16)
    lhs[slot, 1, :, j * cols : (j + 1) * cols] = inner[HALO + x, PAD : PAD + cols, :].astype(BF16).T[:vectors]


def multiply(slot, xs, cols, field, inner, lhs, sums):
    for which, ref in enumerate((field, inner)):
        cells = jnp.concatenate([ref[HALO + x, PAD : PAD + cols, :] for x in xs], axis=0)
        high, low = split(cells)
        sums[which] += jnp.dot(
            lhs[slot, which], jnp.concatenate([high, low], axis=1), preferred_element_type=F32
        )


def middle_kernel(vectors, rows, cols, field_in, stiff, field, odd, inner, turned, sums, lhs):
    tiles = range(PAD - MARGIN, PAD + cols + MARGIN, 8)
    terms = (field, odd)
    for k in range(DEGREE):
        current, following = terms[k % 2], terms[(k + 1) % 2]
        low, high = HALO + 1 + 2 * k, HALO + rows - 1 - 2 * k
        sweep(low, high, tiles, functools.partial(bend, current, stiff, inner))
        sweep(low + 1, high - 1, tiles, functools.partial(advance, k, current, inner, following))
        clear_cols(following, low + 1, high - 1, cols)
    low, high = HALO, rows - HALO
    own = range(PAD, PAD + cols, 8)
    sweep(HALO + low, HALO + high, own, functools.partial(root_bend, terms[DEGREE % 2], stiff, inner))

    first = low + 1
    groups = (high - 1 - first) // GROUP
    sums[...] = jnp.zeros_like(sums)
    final = terms[DEGREE % 2]

    def rows_of(g):
        return [first + g * GROUP + j for j in range(GROUP)]

    def ready(g, slot):
        for j, x in enumerate(rows_of(g)):
            prepare(slot, x, j, vectors, cols, final, inner, turned, lhs)

    ready(0, 0)

    def one(g):
        slot = lax.rem(g, 2)
        multiply(slot, rows_of(g), cols, final, inner, lhs, sums)
        ready(g + 1, 1 - slot)

    loop(groups - 1, one)
    multiply((groups - 1) % 2, rows_of(groups - 1), cols, final, inner, lhs, sums)


def middle(vectors, rows, cols, field, stiff):
    big = padded(rows, cols)
    return pl.pallas_call(
        functools.partial(middle_kernel, vectors, rows, cols),
        in_specs=[VMEM] * 2,
        out_specs=[VMEM] * 5,
        out_shape=[
            big,
            big,
            big,
            jax.ShapeDtypeStruct((rows, vectors, cols), F32),
            jax.ShapeDtypeStruct((2, vectors, 2 * LANES), F32),
        ],
        input_output_aliases={0: 0},
        scratch_shapes=[pltpu.VMEM((2, 2, vectors, GROUP * cols), BF16)],
        compiler_params=params(24),
        cost_estimate=pl.CostEstimate(flops=10**10, bytes_accessed=40 * MIB, transcendentals=0),
    )(field, stiff)


def ends_kernel(vectors, rows, cols, field_in, odd_in, inner_in, stiff_in, turned_in, sums_in,
                one, two, corner_one, corner_two, field, odd, inner, stiff, turned, packed, sums, lhs):
    row_first = even(lax.axis_index("row"))
    base = 2 * HALO * MARGIN

    def fill(start, block, corner):
        for r in range(HALO):
            x = start + r
            weight = corner[base + r : base + r + 1, :]
            field[x, PAD : PAD + cols, :] = lanes_up(block[r * vectors : (r + 1) * vectors, :], weight)
            stiff[x, PAD : PAD + cols, :] = spread_stiffness(weight)
            for e, y in enumerate((PAD - MARGIN, PAD + cols)):
                piece = corner[(2 * r + e) * MARGIN : (2 * r + e + 1) * MARGIN, :]
                field[x, y : y + MARGIN, :] = piece
                stiff[x, y : y + MARGIN, :] = jnp.broadcast_to(
                    piece[:, vectors : vectors + 1] * (2.0 / HALF), (MARGIN, LANES)
                )

    fill(jnp.where(row_first, HALO + rows, 0), one, corner_one)
    fill(jnp.where(row_first, 0, HALO + rows), two, corner_two)

    def both(low, high, start, stop, work):
        tops = ((low, 4), (low + 4, high - low - 4))
        flip = rows + 2 * HALO
        spans = tops + tuple((flip - x - n, n) for x, n in tops)
        wide = 2

        def some(i):
            for u in range(wide):
                y = pl.multiple_of(start + (i * wide + u) * 8, 8)
                for x, n in spans:
                    work(x, y, n)

        loop((stop - start) // (8 * wide), some)

    terms = (field, odd)
    for k in range(DEGREE):
        current, following = terms[k % 2], terms[(k + 1) % 2]
        low = 1 + 2 * k
        span = (PAD - MARGIN, PAD + cols + MARGIN)
        both(low, low + HALO, *span, functools.partial(bend, current, stiff, inner))
        both(low + 1, low + 1 + HALO, *span, functools.partial(advance, k, current, inner, following))
        clear_cols(following, low + 1, low + 1 + HALO, cols)
        clear_cols(following, rows + 2 * HALO - low - 1 - HALO, rows + 2 * HALO - low - 1, cols)
        clear_rows(following, rows, cols)
    final = terms[DEGREE % 2]
    both(HALO, 2 * HALO, PAD, PAD + cols, functools.partial(root_bend, final, stiff, inner))

    sums[...] = sums_in[...]
    xs = list(range(HALO + 1)) + list(range(rows - HALO - 1, rows))
    for g in range(0, len(xs), GROUP):
        for j, x in enumerate(xs[g : g + GROUP]):
            prepare(g // GROUP % 2, x, j, vectors, cols, final, inner, turned, lhs)
        multiply(g // GROUP % 2, xs[g : g + GROUP], cols, final, inner, lhs, sums)

    def total(which):
        high, low = sums[which, :, :LANES], sums[which, :, LANES:]
        square = jnp.concatenate([low, jnp.zeros((LANES - vectors, LANES), F32)], axis=0)
        return high + (low + square.T[:vectors])

    gram, image_gram = total(0), total(1)
    i = lax.broadcasted_iota(jnp.int32, (vectors, LANES), 0)
    j = lax.broadcasted_iota(jnp.int32, (vectors, LANES), 1)
    diagonal = jnp.sum(jnp.where(i == j, image_gram, 0.0), axis=1, keepdims=True)
    both_grams = jnp.where(j <= i, gram, image_gram)
    packed[...] = jnp.where(j < vectors, both_grams, jnp.where(j == vectors, diagonal, 0.0))


def ends(vectors, rows, cols, field, odd, inner, stiff, turned, sums, one, two, corner_one, corner_two):
    big = padded(rows, cols)
    return pl.pallas_call(
        functools.partial(ends_kernel, vectors, rows, cols),
        in_specs=[VMEM] * 10,
        out_specs=[VMEM] * 6,
        out_shape=[
            big,
            big,
            big,
            big,
            jax.ShapeDtypeStruct((rows, vectors, cols), F32),
            jax.ShapeDtypeStruct((vectors, LANES), F32),
        ],
        input_output_aliases={0: 0, 1: 1, 2: 2, 3: 3, 4: 4},
        scratch_shapes=[
            pltpu.VMEM((2, vectors, 2 * LANES), F32),
            pltpu.VMEM((2, 2, vectors, GROUP * cols), BF16),
        ],
        compiler_params=params(24),
    )(field, odd, inner, stiff, turned, sums, one, two, corner_one, corner_two)[4:]


def inverse_factor(gram, vectors):
    lane = lax.broadcasted_iota(jnp.int32, (8, LANES), 1)
    sub = lax.broadcasted_iota(jnp.int32, (8, LANES), 0)
    count = vectors // 8
    blocks = [gram[8 * b : 8 * b + 8] for b in range(count)]

    def spread(values, j):
        return jnp.broadcast_to(values[:, j : j + 1], (8, LANES))

    done = []
    for b in range(count):
        base = 8 * b
        own = (lane >= base) & (lane < base + 8)
        raw = [jnp.broadcast_to(blocks[b][s : s + 1], (8, LANES)) for s in range(8)]
        pivots = [[spread(raw[s], base + k) if k >= s else None for k in range(8)] for s in range(8)]
        below = {t: [spread(blocks[t], base + k) for k in range(8)] for t in range(b + 1, count)}
        rows = [jnp.where(own, jnp.where(lane == base + s, 1.0, 0.0), raw[s]) for s in range(8)]
        for t in range(b + 1, count):
            blocks[t] = jnp.where(own, 0.0, blocks[t])
        finished = jnp.zeros((8, LANES), F32)
        for s in range(8):
            inverse = 1.0 / pivots[s][s]
            for i in range(s + 1, 8):
                m = pivots[s][i] * inverse
                for k in range(i, 8):
                    pivots[i][k] = pivots[i][k] - m * pivots[s][k]
                rows[i] = rows[i] - m * rows[s]
            finished = jnp.where(sub == s, rows[s] * lax.rsqrt(pivots[s][s]), finished)
            for t in range(b + 1, count):
                q = below[t][s] * inverse
                for k in range(s + 1, 8):
                    below[t][k] = below[t][k] - q * pivots[s][k]
                blocks[t] = blocks[t] - q * rows[s]
        done.append(finished)
    full = jnp.concatenate(done, axis=0)
    i = lax.broadcasted_iota(jnp.int32, (vectors, LANES), 0)
    j = lax.broadcasted_iota(jnp.int32, (vectors, LANES), 1)
    return jnp.where(j <= i, full, 0.0)


def finish_kernel(scale, sums_ref, turned, basis_ref, projected_ref, basis, out_sems):
    rows, vectors, cols = turned.shape
    packed = sums_ref[...]
    i = lax.broadcasted_iota(jnp.int32, (vectors, LANES), 0)
    j = lax.broadcasted_iota(jnp.int32, (vectors, LANES), 1)
    square = jnp.concatenate([packed, jnp.zeros((LANES - vectors, LANES), F32)], axis=0)
    flipped = square.T[:vectors]
    gram = jnp.where(j <= i, packed, flipped)
    inverse = inverse_factor(jnp.where(j < vectors, gram, 0.0), vectors)

    high, low = split(inverse[:, :vectors] * scale)
    group = 8
    copies = []
    for x in range(0, rows, group):
        for g in range(0, group, 2):
            pair = jnp.concatenate([turned[x + g], turned[x + g + 1]], axis=1)
            pair_high, pair_low = split(pair)
            result = jnp.dot(high, pair_low, preferred_element_type=F32)
            result += jnp.dot(low, pair_high, preferred_element_type=F32)
            result += jnp.dot(high, pair_high, preferred_element_type=F32)
            basis[:, x + g, :] = result[:, :cols]
            basis[:, x + g + 1, :] = result[:, cols:]
        copies.append(
            pltpu.make_async_copy(
                basis.at[:, pl.ds(x, group), :], basis_ref.at[:, pl.ds(x, group), :], out_sems.at[x // group]
            )
        )
        copies[-1].start()

    image_gram = jnp.where(j > i, packed, jnp.where(j < i, flipped, packed[:, vectors : vectors + 1]))
    image_gram = jnp.where(j < vectors, image_gram, 0.0)
    half = jnp.dot(
        inverse[:, :vectors], image_gram, preferred_element_type=F32, precision=lax.Precision.HIGHEST
    )
    sandwich = lax.dot_general(
        half, inverse, (((1,), (1,)), ((), ())), preferred_element_type=F32, precision=lax.Precision.HIGHEST
    )
    k = lax.broadcasted_iota(jnp.int32, (vectors, vectors), 0)
    m = lax.broadcasted_iota(jnp.int32, (vectors, vectors), 1)
    projected_ref[...] = sandwich * (HALF / (2.0 * TOP)) + jnp.where(k == m, SHIFT / TOP, 0.0)
    for copy in copies:
        copy.wait()


def finish(sums, turned, scale):
    rows, vectors, cols = turned.shape
    return pl.pallas_call(
        functools.partial(finish_kernel, scale),
        in_specs=[VMEM, VMEM],
        out_specs=[HBM, VMEM],
        out_shape=[
            jax.ShapeDtypeStruct((vectors, rows, cols), F32),
            jax.ShapeDtypeStruct((vectors, vectors), F32),
        ],
        scratch_shapes=[
            pltpu.VMEM((vectors, rows, cols), F32),
            pltpu.SemaphoreType.DMA((rows // 8,)),
        ],
        compiler_params=params(24),
    )(sums, turned)


def pairs(count, start):
    found = []
    for i in range(start, count - 1, 2):
        found += [(i, i + 1), (i + 1, i)]
    return found


def all_sum(values, axes):
    count = 1
    for axis in axes:
        count *= lax.axis_size(axis)
    if count & (count - 1):
        return lax.psum(values, axes)
    step = 1
    while step < count:
        values = values + lax.ppermute(values, axes, [(i, i ^ step) for i in range(count)])
        step *= 2
    return values


def body(start_block, stiffness):
    vectors, rows, cols = start_block.shape
    row_count, col_count = lax.axis_size("row"), lax.axis_size("col")
    field, near, far, one, two = turn(start_block, stiffness)
    near = lax.ppermute(near, "col", pairs(col_count, 0))
    far = lax.ppermute(far, "col", pairs(col_count, 1))
    one = lax.ppermute(one, "row", pairs(row_count, 0))
    two = lax.ppermute(two, "row", pairs(row_count, 1))
    stiff = own_stiffness(stiffness, field)
    field, stiff, corner_one, corner_two = corners(vectors, field, stiff, stiffness, near, far)
    corner_one = lax.ppermute(corner_one, "row", pairs(row_count, 0))
    corner_two = lax.ppermute(corner_two, "row", pairs(row_count, 1))
    field, odd, inner, turned, sums = middle(vectors, rows, cols, field, stiff)
    turned, sums = ends(
        vectors, rows, cols, field, odd, inner, stiff, turned, sums, one, two, corner_one, corner_two
    )
    sums = all_sum(sums, ("row", "col"))
    scale = float(rows * row_count * cols * col_count) ** 0.5
    return tuple(finish(sums, turned, scale))


def solution(mesh):
    in_specs = (P(None, "row", "col"), P("row", "col"))
    out_specs = (P(None, "row", "col"), P())
    return jax.shard_map(body, mesh=mesh, in_specs=in_specs, out_specs=out_specs, check_vma=False)
```

profile of v0, /device:TPU:0, one launch (start us, length us, event | category | flops | bytes accessed | tf_op | source)
XLA Modules:
  0.0 73.9 jit_solution(1627343210833049620)
XLA Ops:
  0.6 0.0 copy-start.2
  0.6 1.9 %copy-done.2 = f32[96,64,128]{2,1,0:T(8,128)S(1)} copy-done((f32[96,64,128]{2,1,0:T(8,128)S(1)}, f32[96,64,128]{2,1,0:T(8,128)}, u32[]{:S(2)}) %copy-start.2) | copy-done | bytes 3145752
  2.5 0.0 copy-start.3
  2.5 0.8 %copy-done.3 = f32[64,128]{1,0:T(8,128)S(1)} copy-done((f32[64,128]{1,0:T(8,128)S(1)}, f32[64,128]{1,0:T(8,128)}, u32[]{:S(2)}) %copy-start.3) | copy-done | bytes 32792
  3.3 3.7 %shard_map.41 = (f32[82,160,128]{2,1,0:T(8,128)S(1)}, f32[576,128]{1,0:T(8,128)S(1)}, f32[576,128]{1,0:T(8,128)S(1)}, f32[864,128]{1,0:T(8,128)S(1)}, f32[864,128]{1,0:T(8,128)S(1)}) custom-call(f32[96,64,128]{2,1,0:T(8,128)S(1)} %copy-done.2, f32[64,128]{1,0:T(8,128)S(1)} %copy-done.3), custom_call_target="tpu_custom_call" | custom-call | bytes 6291456 | tf_op jit(solution)/shard_map/pallas_call | solution.py:99
  7.0 0.5 collective-permute-start
  7.5 0.7 collective-permute-start.1
  8.2 2.6 %collective-permute-start.2 = (f32[864,128]{1,0:T(8,128)S(1)}, f32[864,128]{1,0:T(8,128)S(1)}, u32[]{:S(2)}, u32[]{:S(2)}) collective-permute-start(f32[864,128]{1,0:T(8,128)S(1)} %get-tuple-element.28), channel_id=1, source_target_pairs={{0,8},{8,0},{16,24},{24,16},{1,9},{9,1},{17,25},{25,17},{2,10},{10... | collective-permute-start | bytes 1327112 | tf_op jit(solution)/shard_map/ppermute | solution.py:538
  10.8 0.7 collective-permute-start.3
  11.5 1.6 %shard_map.42.stiff_in = f32[82,160,128]{2,1,0:T(8,128)S(1)} custom-call(f32[64,128]{1,0:T(8,128)S(1)} %copy-done.3, f32[82,160,128]{2,1,0:T(8,128)S(1)} %get-tuple-element.18.field.field_in), custom_call_target="tpu_custom_call" | custom-call | bytes 4194304 | tf_op jit(solution)/shard_map/pallas_call | solution.py:127
  13.1 0.0 collective-permute-done.near
  13.1 0.0 collective-permute-done.1.far
  13.1 0.8 %shard_map.43 = (f32[82,160,128]{2,1,0:T(8,128)S(1)}, f32[82,160,128]{2,1,0:T(8,128)S(1)}, f32[160,128]{1,0:T(8,128)S(1)}, f32[160,128]{1,0:T(8,128)S(1)}) custom-call(f32[82,160,128]{2,1,0:T(8,128)S(1)} %get-tuple-element.18.field.field_in, f32[82,160,128]{2,1,0:T(8,128)S(1)} %shard_map.42.stiff_in, ...), custom_call_target="tpu_custom_call", output_to_operand_aliasing={{0}: (0, {}), {1}: (1, {})} | custom-call | tf_op jit(solution)/shard_map/pallas_call | solution.py:172
  13.9 0.0 copy-start
  13.9 2.8 %copy-done = f32[82,160,128]{2,1,0:T(8,128)} copy-done((f32[82,160,128]{2,1,0:T(8,128)}, f32[82,160,128]{2,1,0:T(8,128)S(1)}, u32[]{:S(2)}) %copy-start) | copy-done | bytes 6717464
  16.7 4.2 %collective-permute-start.4 = (f32[160,128]{1,0:T(8,128)S(1)}, f32[160,128]{1,0:T(8,128)S(1)}, u32[]{:S(2)}, u32[]{:S(2)}) collective-permute-start(f32[160,128]{1,0:T(8,128)S(1)} %get-tuple-element.30), channel_id=1, source_target_pairs={{0,8},{8,0},{16,24},{24,16},{1,9},{9,1},{17,25},{25,17},{2,10},{10... | collective-permute-start | bytes 245768 | tf_op jit(solution)/shard_map/ppermute | solution.py:542
  20.9 0.7 collective-permute-start.5
  21.6 0.0 copy-start.1
  21.6 2.9 %copy-done.1 = f32[82,160,128]{2,1,0:T(8,128)S(1)} copy-done((f32[82,160,128]{2,1,0:T(8,128)S(1)}, f32[82,160,128]{2,1,0:T(8,128)}, u32[]{:S(2)}) %copy-start.1) | copy-done | bytes 6717464
  24.5 12.4 %shard_map.44 = (f32[82,160,128]{2,1,0:T(8,128)S(1)}, f32[82,160,128]{2,1,0:T(8,128)S(1)}, f32[82,160,128]{2,1,0:T(8,128)S(1)}, f32[64,96,128]{2,1,0:T(8,128)S(1)}, f32[2,96,256]{2,1,0:T(8,128)S(1)}) custom-call(f32[82,160,128]{2,1,0:T(8,128)S(1)} %get-tuple-element.21.field_in, f32[82,160,128]{2,1,0:T(8,128)S(1)} %copy-done.1), custom_call_target="tpu_custom_call", output_to_operand_aliasing={{0}: (0, {})} | custom-call | flops 10000000000 | bytes 41943040 | tf_op jit(solution)/shard_map/pallas_call | solution.py:301
  36.9 0.0 collective-permute-done.4.corner_one
  36.9 0.0 collective-permute-done.5.corner_two
  36.9 0.0 collective-permute-done.2.one
  36.9 0.0 collective-permute-done.3.two
  36.9 8.5 %shard_map.45 = (f32[82,160,128]{2,1,0:T(8,128)S(1)}, f32[82,160,128]{2,1,0:T(8,128)S(1)}, f32[82,160,128]{2,1,0:T(8,128)S(1)}, f32[82,160,128]{2,1,0:T(8,128)S(...) custom-call(f32[82,160,128]{2,1,0:T(8,128)S(1)} %get-tuple-element.2, ...), custom_call_target="tpu_custom_call", output_to_operand_aliasing={{0}: (0, {}), {1}: (1, {}), {2}: (2, {}), {3}: (3, {}), {4}... | custom-call | tf_op jit(solution)/shard_map/pallas_call | solution.py:389
  45.4 2.1 %collective-permute-start.6 = (f32[96,128]{1,0:T(8,128)S(1)}, f32[96,128]{1,0:T(8,128)S(1)}, u32[]{:S(2)}, u32[]{:S(2)}) collective-permute-start(f32[96,128]{1,0:T(8,128)S(1)} %get-tuple-element.32), channel_id=1, source_target_pairs={{0,1},{1,0},{2,3},{3,2},{4,5},{5,4},{6,7},{7,6},{8,9},{9,8},{10,11... | collective-permute-start | bytes 147464 | tf_op jit(solution)/shard_map/ppermute | solution.py:527
  47.5 0.9 %collective-permute-done.6 = f32[96,128]{1,0:T(8,128)S(1)} collective-permute-done((f32[96,128]{1,0:T(8,128)S(1)}, f32[96,128]{1,0:T(8,128)S(1)}, u32[]{:S(2)}, u32[]{:S(2)}) %collective-permute-start.6) | collective-permute-done | bytes 49184 | tf_op jit(solution)/shard_map/ppermute | solution.py:527
  48.4 1.7 %collective-permute-start.7 = (f32[96,128]{1,0:T(8,128)S(1)}, f32[96,128]{1,0:T(8,128)S(1)}, u32[]{:S(2)}, u32[]{:S(2)}) collective-permute-start(f32[96,128]{1,0:T(8,128)S(1)} %add.15), channel_id=1, source_target_pairs={{0,2},{1,3},{2,0},{3,1},{4,6},{5,7},{6,4},{7,5},{8,10},{9,11},{10,... | collective-permute-start | bytes 147464 | tf_op jit(solution)/shard_map/ppermute | solution.py:527
  50.1 2.4 %collective-permute-done.7 = f32[96,128]{1,0:T(8,128)S(1)} collective-permute-done((f32[96,128]{1,0:T(8,128)S(1)}, f32[96,128]{1,0:T(8,128)S(1)}, u32[]{:S(2)}, u32[]{:S(2)}) %collective-permute-start.7) | collective-permute-done | bytes 49184 | tf_op jit(solution)/shard_map/ppermute | solution.py:527
  52.5 2.7 %collective-permute-start.8 = (f32[96,128]{1,0:T(8,128)S(1)}, f32[96,128]{1,0:T(8,128)S(1)}, u32[]{:S(2)}, u32[]{:S(2)}) collective-permute-start(f32[96,128]{1,0:T(8,128)S(1)} %add.16), channel_id=1, source_target_pairs={{0,4},{1,5},{2,6},{3,7},{4,0},{5,1},{6,2},{7,3},{8,12},{9,13},{10,... | collective-permute-start | bytes 147464 | tf_op jit(solution)/shard_map/ppermute | solution.py:527
  55.2 2.3 %collective-permute-done.8 = f32[96,128]{1,0:T(8,128)S(1)} collective-permute-done((f32[96,128]{1,0:T(8,128)S(1)}, f32[96,128]{1,0:T(8,128)S(1)}, u32[]{:S(2)}, u32[]{:S(2)}) %collective-permute-start.8) | collective-permute-done | bytes 49184 | tf_op jit(solution)/shard_map/ppermute | solution.py:527
  57.5 3.0 %collective-permute-start.9 = (f32[96,128]{1,0:T(8,128)S(1)}, f32[96,128]{1,0:T(8,128)S(1)}, u32[]{:S(2)}, u32[]{:S(2)}) collective-permute-start(f32[96,128]{1,0:T(8,128)S(1)} %add.17), channel_id=1, source_target_pairs={{0,8},{1,9},{2,10},{3,11},{4,12},{5,13},{6,14},{7,15},{8,0},{9,1},... | collective-permute-start | bytes 147464 | tf_op jit(solution)/shard_map/ppermute | solution.py:527
  60.5 2.1 %collective-permute-done.9 = f32[96,128]{1,0:T(8,128)S(1)} collective-permute-done((f32[96,128]{1,0:T(8,128)S(1)}, f32[96,128]{1,0:T(8,128)S(1)}, u32[]{:S(2)}, u32[]{:S(2)}) %collective-permute-start.9) | collective-permute-done | bytes 49184 | tf_op jit(solution)/shard_map/ppermute | solution.py:527
  62.6 1.7 %collective-permute-start.10 = (f32[96,128]{1,0:T(8,128)S(1)}, f32[96,128]{1,0:T(8,128)S(1)}, u32[]{:S(2)}, u32[]{:S(2)}) collective-permute-start(f32[96,128]{1,0:T(8,128)S(1)} %add.18), channel_id=1, source_target_pairs={{0,16},{1,17},{2,18},{3,19},{4,20},{5,21},{6,22},{7,23},{8,24},{9,... | collective-permute-start | bytes 147464 | tf_op jit(solution)/shard_map/ppermute | solution.py:527
  64.3 2.5 %collective-permute-done.10 = f32[96,128]{1,0:T(8,128)S(1)} collective-permute-done((f32[96,128]{1,0:T(8,128)S(1)}, f32[96,128]{1,0:T(8,128)S(1)}, u32[]{:S(2)}, u32[]{:S(2)}) %collective-permute-start.10) | collective-permute-done | bytes 49184 | tf_op jit(solution)/shard_map/ppermute | solution.py:527
  66.8 7.1 %shard_map.46 = (f32[96,64,128]{2,1,0:T(8,128)}, f32[96,96]{1,0:T(8,128)}) custom-call(f32[96,128]{1,0:T(8,128)S(1)} %add.19.sums_ref, f32[64,96,128]{2,1,0:T(8,128)S(1)} %get-tuple-element.33.turned), custom_call_target="tpu_custom_call" | custom-call | tf_op jit(solution)/shard_map/pallas_call | solution.py:496
  (5 shorter events, 0.0 us)
Async XLA Ops:
  0.6 1.9 %copy-start.2 = (f32[96,64,128]{2,1,0:T(8,128)S(1)}, f32[96,64,128]{2,1,0:T(8,128)}, u32[]{:S(2)}) copy-start(f32[96,64,128]{2,1,0:T(8,128)} %block_ref.1) | copy-start | bytes 9437188
  2.5 0.8 %copy-start.3 = (f32[64,128]{1,0:T(8,128)S(1)}, f32[64,128]{1,0:T(8,128)}, u32[]{:S(2)}) copy-start(f32[64,128]{1,0:T(8,128)} %stiff_ref.5) | copy-start | bytes 98308
  7.0 6.1 %collective-permute-start = (f32[576,128]{1,0:T(8,128)S(1)}, f32[576,128]{1,0:T(8,128)S(1)}, u32[]{:S(2)}, u32[]{:S(2)}) collective-permute-start(f32[576,128]{1,0:T(8,128)S(1)} %get-tuple-element.19), channel_id=1, source_target_pairs={{0,1},{1,0},{2,3},{3,2},{4,5},{5,4},{6,7},{7,6},{8,9},{9,8},{10,11... | collective-permute-start | bytes 884744 | tf_op jit(solution)/shard_map/ppermute | solution.py:536
  7.5 5.6 %collective-permute-start.1 = (f32[576,128]{1,0:T(8,128)S(1)}, f32[576,128]{1,0:T(8,128)S(1)}, u32[]{:S(2)}, u32[]{:S(2)}) collective-permute-start(f32[576,128]{1,0:T(8,128)S(1)} %get-tuple-element.20), channel_id=1, source_target_pairs={{1,2},{2,1},{3,4},{4,3},{5,6},{6,5},{9,10},{10,9},{11,12},{12,11},... | collective-permute-start | bytes 884744 | tf_op jit(solution)/shard_map/ppermute | solution.py:537
  8.2 28.7 %collective-permute-start.2 = (f32[864,128]{1,0:T(8,128)S(1)}, f32[864,128]{1,0:T(8,128)S(1)}, u32[]{:S(2)}, u32[]{:S(2)}) collective-permute-start(f32[864,128]{1,0:T(8,128)S(1)} %get-tuple-element.28), channel_id=1, source_target_pairs={{0,8},{8,0},{16,24},{24,16},{1,9},{9,1},{17,25},{25,17},{2,10},{10... | collective-permute-start | bytes 1327112 | tf_op jit(solution)/shard_map/ppermute | solution.py:538
  10.8 26.1 %collective-permute-start.3 = (f32[864,128]{1,0:T(8,128)S(1)}, f32[864,128]{1,0:T(8,128)S(1)}, u32[]{:S(2)}, u32[]{:S(2)}) collective-permute-start(f32[864,128]{1,0:T(8,128)S(1)} %get-tuple-element.29), channel_id=1, source_target_pairs={{8,16},{16,8},{9,17},{17,9},{10,18},{18,10},{11,19},{19,11},{12,20... | collective-permute-start | bytes 1327112 | tf_op jit(solution)/shard_map/ppermute | solution.py:539
  13.9 2.8 %copy-start = (f32[82,160,128]{2,1,0:T(8,128)}, f32[82,160,128]{2,1,0:T(8,128)S(1)}, u32[]{:S(2)}) copy-start(f32[82,160,128]{2,1,0:T(8,128)S(1)} %get-tuple-element.22.stiff.stiff_in) | copy-start | bytes 20152324
  16.7 20.2 %collective-permute-start.4 = (f32[160,128]{1,0:T(8,128)S(1)}, f32[160,128]{1,0:T(8,128)S(1)}, u32[]{:S(2)}, u32[]{:S(2)}) collective-permute-start(f32[160,128]{1,0:T(8,128)S(1)} %get-tuple-element.30), channel_id=1, source_target_pairs={{0,8},{8,0},{16,24},{24,16},{1,9},{9,1},{17,25},{25,17},{2,10},{10... | collective-permute-start | bytes 245768 | tf_op jit(solution)/shard_map/ppermute | solution.py:542
  20.9 16.0 %collective-permute-start.5 = (f32[160,128]{1,0:T(8,128)S(1)}, f32[160,128]{1,0:T(8,128)S(1)}, u32[]{:S(2)}, u32[]{:S(2)}) collective-permute-start(f32[160,128]{1,0:T(8,128)S(1)} %get-tuple-element.31), channel_id=1, source_target_pairs={{8,16},{16,8},{9,17},{17,9},{10,18},{18,10},{11,19},{19,11},{12,20... | collective-permute-start | bytes 245768 | tf_op jit(solution)/shard_map/ppermute | solution.py:543
  21.6 2.9 %copy-start.1 = (f32[82,160,128]{2,1,0:T(8,128)S(1)}, f32[82,160,128]{2,1,0:T(8,128)}, u32[]{:S(2)}) copy-start(f32[82,160,128]{2,1,0:T(8,128)} %copy-done) | copy-start | bytes 20152324
  45.4 3.0 %collective-permute-start.6 = (f32[96,128]{1,0:T(8,128)S(1)}, f32[96,128]{1,0:T(8,128)S(1)}, u32[]{:S(2)}, u32[]{:S(2)}) collective-permute-start(f32[96,128]{1,0:T(8,128)S(1)} %get-tuple-element.32), channel_id=1, source_target_pairs={{0,1},{1,0},{2,3},{3,2},{4,5},{5,4},{6,7},{7,6},{8,9},{9,8},{10,11... | collective-permute-start | bytes 147464 | tf_op jit(solution)/shard_map/ppermute | solution.py:527
  48.4 4.1 %collective-permute-start.7 = (f32[96,128]{1,0:T(8,128)S(1)}, f32[96,128]{1,0:T(8,128)S(1)}, u32[]{:S(2)}, u32[]{:S(2)}) collective-permute-start(f32[96,128]{1,0:T(8,128)S(1)} %add.15), channel_id=1, source_target_pairs={{0,2},{1,3},{2,0},{3,1},{4,6},{5,7},{6,4},{7,5},{8,10},{9,11},{10,... | collective-permute-start | bytes 147464 | tf_op jit(solution)/shard_map/ppermute | solution.py:527
  52.5 5.0 %collective-permute-start.8 = (f32[96,128]{1,0:T(8,128)S(1)}, f32[96,128]{1,0:T(8,128)S(1)}, u32[]{:S(2)}, u32[]{:S(2)}) collective-permute-start(f32[96,128]{1,0:T(8,128)S(1)} %add.16), channel_id=1, source_target_pairs={{0,4},{1,5},{2,6},{3,7},{4,0},{5,1},{6,2},{7,3},{8,12},{9,13},{10,... | collective-permute-start | bytes 147464 | tf_op jit(solution)/shard_map/ppermute | solution.py:527
  57.5 5.1 %collective-permute-start.9 = (f32[96,128]{1,0:T(8,128)S(1)}, f32[96,128]{1,0:T(8,128)S(1)}, u32[]{:S(2)}, u32[]{:S(2)}) collective-permute-start(f32[96,128]{1,0:T(8,128)S(1)} %add.17), channel_id=1, source_target_pairs={{0,8},{1,9},{2,10},{3,11},{4,12},{5,13},{6,14},{7,15},{8,0},{9,1},... | collective-permute-start | bytes 147464 | tf_op jit(solution)/shard_map/ppermute | solution.py:527
  62.6 4.2 %collective-permute-start.10 = (f32[96,128]{1,0:T(8,128)S(1)}, f32[96,128]{1,0:T(8,128)S(1)}, u32[]{:S(2)}, u32[]{:S(2)}) collective-permute-start(f32[96,128]{1,0:T(8,128)S(1)} %add.18), channel_id=1, source_target_pairs={{0,16},{1,17},{2,18},{3,19},{4,20},{5,21},{6,22},{7,23},{8,24},{9,... | collective-permute-start | bytes 147464 | tf_op jit(solution)/shard_map/ppermute | solution.py:527
where the time goes:
time: 74.2 us; the launch traced here: 73.9 us
  Pallas kernels  34.1 us (46%)
  starting transfers between devices  20.5 us (28%)
  waiting for transfers between devices  10.1 us (14%)
  local copies, waits for them, and re-layouts  8.34 us (11%)
  between operations  0.77 us (1%)
    pallas_call x1, Pallas kernels, middle(): pl.pallas_call(functools.partial(middle_kernel, vectors, rows, cols), in_...  12.4 us
    ppermute x5, starting transfers between devices, all_sum(): lax.ppermute(values, axes, [(i, i ^ step) for i in range(count)])  11.2 us
    ppermute x5, waiting for transfers between devices, all_sum(): lax.ppermute(values, axes, [(i, i ^ step) for i in range(count)])  10.1 us
    pallas_call x1, Pallas kernels, ends(): pl.pallas_call(functools.partial(ends_kernel, vectors, rows, cols), in_sp...  8.45 us
    unnamed x8, local copies, waits for them, and re-layouts  8.34 us
    pallas_call x1, Pallas kernels, finish(): pl.pallas_call(functools.partial(finish_kernel, scale), in_specs=[VMEM, V...  7.11 us
    ppermute x1, starting transfers between devices, body(): corner_one = lax.ppermute(corner_one, 'row', pairs(row_count, 0))  4.2 us
    pallas_call x1, Pallas kernels, turn(): pl.pallas_call(turn_kernel, in_specs=[HBM, VMEM], out_specs=[VMEM] * 5, o...  3.72 us
  transfers between devices with their start and end apart: 11, of which 5 were waited for; matrix products, arithmetic and copies ran while one was open for 0% of the time, Pallas kernels for 20%

commit v1 on v0

--- a/solution.py
+++ b/solution.py
@@ -15,6 +15,8 @@
 LEAD = (CENTER - SHIFT) / HALF
 HALO = 2 * DEGREE + 1
 MARGIN = HALO - 1
+FIRST = 5
+EARLY = 1
 LANES = 128
 PAD = 16
 GROUP = 4
@@ -22,7 +24,7 @@
 BF16 = jnp.bfloat16
 MIB = 2**20
 VMEM = pl.BlockSpec(memory_space=pltpu.VMEM)
-HBM = pl.BlockSpec(memory_space=pl.ANY)
+HBM = pl.BlockSpec(memory_space=pltpu.HBM)
 
 
 def split(values):
@@ -61,80 +63,77 @@
     return jnp.broadcast_to(row * (2.0 / HALF), (LANES, row.shape[1])).T
 
 
-def turn_kernel(block_ref, stiff_ref, field, near, far, one, two, held, sems):
+def turn_kernel(block_ref, stiff_ref, field, near, far, one, two, rest, stiff, held, sems, slab_sems):
     chunks, vectors, step, cols = held.shape
     rows = chunks * step
     col_first, row_first = even(lax.axis_index("col")), even(lax.axis_index("row"))
+    stiff_copy = pltpu.make_async_copy(stiff_ref, stiff, sems.at[chunks])
     copies = [
         pltpu.make_async_copy(block_ref.at[:, pl.ds(i * step, step), :], held.at[i], sems.at[i])
         for i in range(chunks)
     ]
-    for copy in copies:
+    slab_copies = []
+    for which, start in enumerate(
+        (jnp.where(row_first, rows - HALO, 0), jnp.where(row_first, 0, rows - HALO))
+    ):
+        for r in range(HALO):
+            out, at = (one, r) if which == 0 else (two, r) if r < FIRST else (rest, r - FIRST)
+            slab_copies.append(
+                pltpu.make_async_copy(
+                    block_ref.at[:, start + r, :], out.at[pl.ds(at * vectors, vectors), :], slab_sems.at[which, r]
+                )
+            )
+    for copy in [stiff_copy] + copies + slab_copies:
         copy.start()
-
-    def chunk(i):
-        pltpu.make_async_copy(block_ref.at[:, pl.ds(i * step, step), :], held.at[i], sems.at[i]).wait()
+    stiff_copy.wait()
+    for i in range(chunks):
+        copies[i].wait()
         for r in range(step):
             x = i * step + r
-            turned = lanes_up(held[i, :, r, :], stiff_ref[pl.ds(x, 1), :])
+            turned = lanes_up(held[i, :, r, :], stiff[x : x + 1, :])
             field[HALO + x, PAD : PAD + cols, :] = turned
             head, tail = turned[:HALO], turned[cols - HALO :]
-            near[pl.ds(x * HALO, HALO), :] = jnp.where(col_first, tail, head)
-            far[pl.ds(x * HALO, HALO), :] = jnp.where(col_first, head, tail)
-
-    loop(chunks, chunk)
-    for r in range(HALO):
-        end = rows - HALO + r
-        head = held[r // step, :, r % step, :]
-        tail = held[end // step, :, end % step, :]
-        one[r * vectors : (r + 1) * vectors, :] = jnp.where(row_first, tail, head)
-        two[r * vectors : (r + 1) * vectors, :] = jnp.where(row_first, head, tail)
+            near[x * HALO : (x + 1) * HALO, :] = jnp.where(col_first, tail, head)
+            far[x * HALO : (x + 1) * HALO, :] = jnp.where(col_first, head, tail)
+    for copy in slab_copies:
+        copy.wait()
 
 
 def turn(block, stiffness):
     vectors, rows, cols = block.shape
     side = jax.ShapeDtypeStruct((rows * HALO, LANES), F32)
-    end = jax.ShapeDtypeStruct((HALO * vectors, cols), F32)
-    step = 8
+
+    def slab(count):
+        return jax.ShapeDtypeStruct((count * vectors, cols), F32)
+
+    step = 16
     return pl.pallas_call(
         turn_kernel,
-        in_specs=[HBM, VMEM],
-        out_specs=[VMEM] * 5,
-        out_shape=[padded(rows, cols), side, side, end, end],
+        in_specs=[HBM] * 2,
+        out_specs=[VMEM] * 7,
+        out_shape=[
+            padded(rows, cols),
+            side,
+            side,
+            slab(HALO),
+            slab(FIRST),
+            slab(HALO - FIRST),
+            jax.ShapeDtypeStruct(stiffness.shape, F32),
+        ],
         scratch_shapes=[
             pltpu.VMEM((rows // step, vectors, step, cols), F32),
-            pltpu.SemaphoreType.DMA((rows // step,)),
+            pltpu.SemaphoreType.DMA((rows // step + 1,)),
+            pltpu.SemaphoreType.DMA((2, HALO)),
         ],
-        compiler_params=params(24),
+        compiler_params=params(8),
         cost_estimate=pl.CostEstimate(flops=0, bytes_accessed=4 * vectors * rows * cols * 2, transcendentals=0),
-    )(block, stiffness)
-
-
-def stiff_kernel(stiff_ref, field, stiff):
-    rows, cols = stiff_ref.shape
-    step = 8
-
-    def some(i):
-        for r in range(step):
-            x = i * step + r
-            stiff[HALO + x, PAD : PAD + cols, :] = spread_stiffness(stiff_ref[pl.ds(x, 1), :])
-
-    loop(rows // step, some)
-
-
-def own_stiffness(stiffness, field):
-    rows, cols = stiffness.shape
-    return pl.pallas_call(
-        stiff_kernel,
-        in_specs=[VMEM, HBM],
-        out_specs=VMEM,
-        out_shape=padded(rows, cols),
-        compiler_params=params(16),
-        cost_estimate=pl.CostEstimate(flops=0, bytes_accessed=4 * LANES * rows * cols, transcendentals=0),
-    )(stiffness, field)
-
-
-def corner_kernel(vectors, field_in, stiff_in, stiff_ref, near, far, field, stiff, one, two):
+    )(
+        pltpu.with_memory_space_constraint(block, pltpu.HBM),
+        pltpu.with_memory_space_constraint(stiffness, pltpu.HBM),
+    )
+
+
+def corner_kernel(vectors, field_in, stiff_in, stiff_ref, near, far, rest, field, stiff, one, whole):
     rows, cols = stiff_ref.shape
     col_first, row_first = even(lax.axis_index("col")), even(lax.axis_index("row"))
     step = 8
@@ -154,6 +153,9 @@
 
     loop(rows // step, some)
     last = rows - HALO
+    size = rest.shape[0]
+    whole[:size, :] = rest[...]
+    two = whole.at[size:, :]
     for out, start in ((one, jnp.where(row_first, last, 0)), (two, jnp.where(row_first, 0, last))):
         for r in range(HALO):
             for e, y in enumerate(ends):
@@ -166,17 +168,19 @@
     two[base : base + HALO, :] = jnp.where(row_first, head, tail)
 
 
-def corners(vectors, field, stiff, stiffness, near, far):
+def corners(vectors, field, stiff, stiffness, near, far, rest):
     rows, cols = stiffness.shape
     corner = jax.ShapeDtypeStruct((2 * HALO * MARGIN + 16, LANES), F32)
+    whole = jax.ShapeDtypeStruct((rest.shape[0] + corner.shape[0], LANES), F32)
     return pl.pallas_call(
         functools.partial(corner_kernel, vectors),
-        in_specs=[VMEM] * 5,
+        in_specs=[VMEM] * 6,
         out_specs=[VMEM] * 4,
-        out_shape=[padded(rows, cols), padded(rows, cols), corner, corner],
+        out_shape=[padded(rows, cols), padded(rows, cols), corner, whole],
         input_output_aliases={0: 0, 1: 1},
-        compiler_params=params(16),
-    )(field, stiff, stiffness, near, far)
+        compiler_params=params(4),
+        cost_estimate=pl.CostEstimate(flops=0, bytes_accessed=0, transcendentals=0),
+    )(field, stiff, stiffness, near, far, rest)
 
 
 def around(ref, x, y, step):
@@ -208,18 +212,18 @@
 
 
 def sweep(low, high, ys, work):
-    step = 4
-    whole = (high - low) // step
-
-    def chunk(i):
+    step, unroll = 4, 4
+
+    def trip(i):
+        for u in range(unroll):
+            for y in ys:
+                work(low + (i * unroll + u) * step, y, step)
+
+    trips = (high - low) // (step * unroll)
+    loop(trips, trip)
+    for x in range(low + trips * unroll * step, high, step):
         for y in ys:
-            work(low + i * step, y, step)
-
-    loop(whole, chunk)
-    rest = (high - low) - whole * step
-    if rest:
-        for y in ys:
-            work(high - rest, y, rest)
+            work(x, y, min(step, high - x))
 
 
 def clear_cols(field, low, high, cols):
@@ -242,6 +246,45 @@
 
     pl.when(row == 0)(lambda: at(0))
     pl.when(row == count - 1)(lambda: at(HALO + rows))
+
+
+def tiles_of(cols, inset):
+    return range(PAD - MARGIN + 8 * inset, PAD + cols + MARGIN - 8 * inset, 8)
+
+
+def operator(k, rows, bends, advances, field, odd, inner, stiff):
+    current, following = ((field, odd), (odd, field))[k % 2]
+    low, high = HALO + 1 + 2 * k, HALO + rows - 1 - 2 * k
+    sweep(low, high, bends, functools.partial(bend, current, stiff, inner))
+    sweep(low + 1, high - 1, advances, functools.partial(advance, k, current, inner, following))
+
+
+def early_kernel(field_in, stiff_ref, field, stiff, odd, inner):
+    rows, cols = stiff_ref.shape
+    step = 8
+
+    def some(i):
+        for r in range(step):
+            x = i * step + r
+            stiff[HALO + x, PAD : PAD + cols, :] = spread_stiffness(stiff_ref[pl.ds(x, 1), :])
+
+    loop(rows // step, some)
+    for k in range(EARLY):
+        operator(k, rows, tiles_of(cols, 2 * k + 2), tiles_of(cols, 2 * k + 3), field, odd, inner, stiff)
+
+
+def early(field, stiffness):
+    rows, cols = stiffness.shape
+    big = padded(rows, cols)
+    return pl.pallas_call(
+        early_kernel,
+        in_specs=[VMEM] * 2,
+        out_specs=[VMEM] * 4,
+        out_shape=[big] * 4,
+        input_output_aliases={0: 0},
+        compiler_params=params(4),
+        cost_estimate=pl.CostEstimate(flops=0, bytes_accessed=0, transcendentals=0),
+    )(field, stiffness)
 
 
 def prepare(slot, x, j, vectors, cols, field, inner, turned, lhs):
@@ -260,15 +303,20 @@
         )
 
 
-def middle_kernel(vectors, rows, cols, field_in, stiff, field, odd, inner, turned, sums, lhs):
-    tiles = range(PAD - MARGIN, PAD + cols + MARGIN, 8)
+def middle_kernel(vectors, rows, cols, field_in, odd_in, inner_in, stiff_in, one, field, odd, inner, stiff, turned, sums, lhs):
+    outside = jnp.where(even(lax.axis_index("row")), HALO + rows, 0)
+    for r in range(HALO):
+        block = one[r * vectors : (r + 1) * vectors, :]
+        field[outside + r, PAD : PAD + cols, :] = lanes_up(block, jnp.zeros((1, cols), F32))
     terms = (field, odd)
     for k in range(DEGREE):
-        current, following = terms[k % 2], terms[(k + 1) % 2]
-        low, high = HALO + 1 + 2 * k, HALO + rows - 1 - 2 * k
-        sweep(low, high, tiles, functools.partial(bend, current, stiff, inner))
-        sweep(low + 1, high - 1, tiles, functools.partial(advance, k, current, inner, following))
-        clear_cols(following, low + 1, high - 1, cols)
+        tiles = tiles_of(cols, 0)
+        bends = advances = tiles
+        if k < EARLY:
+            bends = [y for y in tiles if y not in tiles_of(cols, 2 * k + 2)]
+            advances = [y for y in tiles if y not in tiles_of(cols, 2 * k + 3)]
+        operator(k, rows, bends, advances, field, odd, inner, stiff)
+        clear_cols(terms[(k + 1) % 2], HALO + 2 + 2 * k, HALO + rows - 2 - 2 * k, cols)
     low, high = HALO, rows - HALO
     own = range(PAD, PAD + cols, 8)
     sweep(HALO + low, HALO + high, own, functools.partial(root_bend, terms[DEGREE % 2], stiff, inner))
@@ -296,36 +344,38 @@
     multiply((groups - 1) % 2, rows_of(groups - 1), cols, final, inner, lhs, sums)
 
 
-def middle(vectors, rows, cols, field, stiff):
+def middle(vectors, rows, cols, field, odd, inner, stiff, one):
     big = padded(rows, cols)
     return pl.pallas_call(
         functools.partial(middle_kernel, vectors, rows, cols),
-        in_specs=[VMEM] * 2,
-        out_specs=[VMEM] * 5,
+        in_specs=[VMEM] * 5,
+        out_specs=[VMEM] * 6,
         out_shape=[
+            big,
             big,
             big,
             big,
             jax.ShapeDtypeStruct((rows, vectors, cols), F32),
             jax.ShapeDtypeStruct((2, vectors, 2 * LANES), F32),
         ],
-        input_output_aliases={0: 0},
+        input_output_aliases={0: 0, 1: 1, 2: 2, 3: 3},
         scratch_shapes=[pltpu.VMEM((2, 2, vectors, GROUP * cols), BF16)],
-        compiler_params=params(24),
+        compiler_params=params(8),
         cost_estimate=pl.CostEstimate(flops=10**10, bytes_accessed=40 * MIB, transcendentals=0),
-    )(field, stiff)
+    )(field, odd, inner, stiff, one)
 
 
 def ends_kernel(vectors, rows, cols, field_in, odd_in, inner_in, stiff_in, turned_in, sums_in,
-                one, two, corner_one, corner_two, field, odd, inner, stiff, turned, packed, sums, lhs):
+                two, corner_one, whole, field, odd, inner, stiff, turned, packed, sums, lhs):
     row_first = even(lax.axis_index("row"))
     base = 2 * HALO * MARGIN
 
-    def fill(start, block, corner):
+    def fill(start, row_block, corner):
         for r in range(HALO):
             x = start + r
             weight = corner[base + r : base + r + 1, :]
-            field[x, PAD : PAD + cols, :] = lanes_up(block[r * vectors : (r + 1) * vectors, :], weight)
+            if row_block is not None:
+                field[x, PAD : PAD + cols, :] = lanes_up(row_block(r), weight)
             stiff[x, PAD : PAD + cols, :] = spread_stiffness(weight)
             for e, y in enumerate((PAD - MARGIN, PAD + cols)):
                 piece = corner[(2 * r + e) * MARGIN : (2 * r + e + 1) * MARGIN, :]
@@ -334,35 +384,36 @@
                     piece[:, vectors : vectors + 1] * (2.0 / HALF), (MARGIN, LANES)
                 )
 
-    fill(jnp.where(row_first, HALO + rows, 0), one, corner_one)
-    fill(jnp.where(row_first, 0, HALO + rows), two, corner_two)
-
-    def both(low, high, start, stop, work):
-        tops = ((low, 4), (low + 4, high - low - 4))
+    def second(r):
+        ref, at = (two, r) if r < FIRST else (whole, r - FIRST)
+        return ref[at * vectors : (at + 1) * vectors, :]
+
+    fill(jnp.where(row_first, HALO + rows, 0), None, corner_one)
+    fill(jnp.where(row_first, 0, HALO + rows), second, whole.at[(HALO - FIRST) * vectors :, :])
+
+    def both(low, high, ys, work):
         flip = rows + 2 * HALO
-        spans = tops + tuple((flip - x - n, n) for x, n in tops)
-        wide = 2
-
-        def some(i):
-            for u in range(wide):
-                y = pl.multiple_of(start + (i * wide + u) * 8, 8)
-                for x, n in spans:
-                    work(x, y, n)
-
-        loop((stop - start) // (8 * wide), some)
+
+        def side(i):
+            x = low + i * (flip - high - low)
+            for y in ys:
+                work(x, y, 4)
+                work(x + 4, y, high - low - 4)
+
+        loop(2, side)
 
     terms = (field, odd)
     for k in range(DEGREE):
         current, following = terms[k % 2], terms[(k + 1) % 2]
         low = 1 + 2 * k
-        span = (PAD - MARGIN, PAD + cols + MARGIN)
-        both(low, low + HALO, *span, functools.partial(bend, current, stiff, inner))
-        both(low + 1, low + 1 + HALO, *span, functools.partial(advance, k, current, inner, following))
+        tiles = tiles_of(cols, 0)
+        both(low, low + HALO, tiles, functools.partial(bend, current, stiff, inner))
+        both(low + 1, low + 1 + HALO, tiles, functools.partial(advance, k, current, inner, following))
         clear_cols(following, low + 1, low + 1 + HALO, cols)
         clear_cols(following, rows + 2 * HALO - low - 1 - HALO, rows + 2 * HALO - low - 1, cols)
         clear_rows(following, rows, cols)
     final = terms[DEGREE % 2]
-    both(HALO, 2 * HALO, PAD, PAD + cols, functools.partial(root_bend, final, stiff, inner))
+    both(HALO, 2 * HALO, tiles_of(cols, 1), functools.partial(root_bend, final, stiff, inner))
 
     sums[...] = sums_in[...]
     xs = list(range(HALO + 1)) + list(range(rows - HALO - 1, rows))
@@ -384,11 +435,11 @@
     packed[...] = jnp.where(j < vectors, both_grams, jnp.where(j == vectors, diagonal, 0.0))
 
 
-def ends(vectors, rows, cols, field, odd, inner, stiff, turned, sums, one, two, corner_one, corner_two):
+def ends(vectors, rows, cols, field, odd, inner, stiff, turned, sums, two, corner_one, whole):
     big = padded(rows, cols)
     return pl.pallas_call(
         functools.partial(ends_kernel, vectors, rows, cols),
-        in_specs=[VMEM] * 10,
+        in_specs=[VMEM] * 9,
         out_specs=[VMEM] * 6,
         out_shape=[
             big,
@@ -403,8 +454,8 @@
             pltpu.VMEM((2, vectors, 2 * LANES), F32),
             pltpu.VMEM((2, 2, vectors, GROUP * cols), BF16),
         ],
-        compiler_params=params(24),
-    )(field, odd, inner, stiff, turned, sums, one, two, corner_one, corner_two)[4:]
+        compiler_params=params(8),
+    )(field, odd, inner, stiff, turned, sums, two, corner_one, whole)[4:]
 
 
 def inverse_factor(gram, vectors):
@@ -505,7 +556,7 @@
             pltpu.VMEM((vectors, rows, cols), F32),
             pltpu.SemaphoreType.DMA((rows // 8,)),
         ],
-        compiler_params=params(24),
+        compiler_params=params(8),
     )(sums, turned)
 
 
@@ -532,19 +583,17 @@
 def body(start_block, stiffness):
     vectors, rows, cols = start_block.shape
     row_count, col_count = lax.axis_size("row"), lax.axis_size("col")
-    field, near, far, one, two = turn(start_block, stiffness)
+    field, near, far, one, two, rest, stiffness = turn(start_block, stiffness)
     near = lax.ppermute(near, "col", pairs(col_count, 0))
     far = lax.ppermute(far, "col", pairs(col_count, 1))
     one = lax.ppermute(one, "row", pairs(row_count, 0))
     two = lax.ppermute(two, "row", pairs(row_count, 1))
-    stiff = own_stiffness(stiffness, field)
-    field, stiff, corner_one, corner_two = corners(vectors, field, stiff, stiffness, near, far)
+    field, stiff, odd, inner = early(field, stiffness)
+    field, stiff, corner_one, whole = corners(vectors, field, stiff, stiffness, near, far, rest)
     corner_one = lax.ppermute(corner_one, "row", pairs(row_count, 0))
-    corner_two = lax.ppermute(corner_two, "row", pairs(row_count, 1))
-    field, odd, inner, turned, sums = middle(vectors, rows, cols, field, stiff)
-    turned, sums = ends(
-        vectors, rows, cols, field, odd, inner, stiff, turned, sums, one, two, corner_one, corner_two
-    )
+    whole = lax.ppermute(whole, "row", pairs(row_count, 1))
+    field, odd, inner, stiff, turned, sums = middle(vectors, rows, cols, field, odd, inner, stiff, one)
+    turned, sums = ends(vectors, rows, cols, field, odd, inner, stiff, turned, sums, two, corner_one, whole)
     sums = all_sum(sums, ("row", "col"))
     scale = float(rows * row_count * cols * col_count) ** 0.5
     return tuple(finish(sums, turned, scale))

time: 74.2 us -> 63.1 us (0.85)
  local copies, waits for them, and re-layouts: 8.34 us -> 0 us
  Pallas kernels: 34.1 us -> 30.9 us
  waiting for transfers between devices: 10.1 us -> 11 us
    unnamed x8 -> x0, local copies, waits for them, and re-layouts: 8.34 us -> none
    pallas_call x1, Pallas kernels: 8.45 us -> 5.59 us  [ends(): pl.pallas_call(functools.partial(ends_kernel, vectors, rows, cols), in_sp...]
    pallas_call x1, Pallas kernels: 12.4 us -> 10.4 us  [middle(): pl.pallas_call(functools.partial(middle_kernel, vectors, rows, cols), in_...]
    pallas_call x2, Pallas kernels: 5.35 us -> 7.09 us  [the longest x1 3.89 us: turn(): pl.pallas_call(turn_kernel, in_specs=[HBM] * 2, out_specs=[VMEM] * 7, out...]
  transfers between devices with their start and end apart: 11 -> 11, of which waited for: 5 -> 6; matrix products, arithmetic and copies ran while one was open for 0% -> 0% of each run, Pallas kernels for 20% -> 23%
where the time goes in v1:
time: 63.1 us; the launch traced here: 62.9 us
  Pallas kernels  30.9 us (49%)
  starting transfers between devices  20 us (32%)
  waiting for transfers between devices  11 us (17%)
  between operations  0.9 us (1%)
    ppermute x5, starting transfers between devices, all_sum(): lax.ppermute(values, axes, [(i, i ^ step) for i in range(count)])  10.7 us
    ppermute x5, waiting for transfers between devices, all_sum(): lax.ppermute(values, axes, [(i, i ^ step) for i in range(count)])  10.4 us
    pallas_call x1, Pallas kernels, middle(): pl.pallas_call(functools.partial(middle_kernel, vectors, rows, cols), in_...  10.4 us
    pallas_call x1, Pallas kernels, finish(): pl.pallas_call(functools.partial(finish_kernel, scale), in_specs=[VMEM, V...  7.11 us
    pallas_call x1, Pallas kernels, ends(): pl.pallas_call(functools.partial(ends_kernel, vectors, rows, cols), in_sp...  5.59 us
    ppermute x1, starting transfers between devices, body(): corner_one = lax.ppermute(corner_one, 'row', pairs(row_count, 0))  4.28 us
    pallas_call x1, Pallas kernels, turn(): pl.pallas_call(turn_kernel, in_specs=[HBM] * 2, out_specs=[VMEM] * 7, out...  3.89 us
    pallas_call x1, Pallas kernels, early(): pl.pallas_call(early_kernel, in_specs=[VMEM] * 2, out_specs=[VMEM] * 4, o...  3.2 us
  transfers between devices with their start and end apart: 11, of which 6 were waited for; matrix products, arithmetic and copies ran while one was open for 0% of the time, Pallas kernels for 23%

profile of v1, /device:TPU:0, one launch (start us, length us, event | category | flops | bytes accessed | tf_op | source)
XLA Modules:
  0.0 62.9 jit_solution(16721698939458532337)
XLA Ops:
  0.6 3.9 %shard_map.41 = (f32[82,160,128]{2,1,0:T(8,128)S(1)}, f32[576,128]{1,0:T(8,128)S(1)}, f32[576,128]{1,0:T(8,128)S(1)}, f32[864,128]{1,0:T(8,128)S(1)}, f32[480,12...) custom-call(f32[96,64,128]{2,1,0:T(8,128)} %block_ref.1, f32[64,128]{1,0:T(8,128)} %stiff_ref.1), custom_call_target="tpu_custom_call" | custom-call | bytes 6291456 | tf_op jit(solution)/shard_map/pallas_call | solution.py:110
  4.5 3.0 %collective-permute-start.2 = (f32[864,128]{1,0:T(8,128)S(1)}, f32[864,128]{1,0:T(8,128)S(1)}, u32[]{:S(2)}, u32[]{:S(2)}) collective-permute-start(f32[864,128]{1,0:T(8,128)S(1)} %get-tuple-element.36), channel_id=1, source_target_pairs={{0,8},{8,0},{16,24},{24,16},{1,9},{9,1},{17,25},{25,17},{2,10},{10... | collective-permute-start | bytes 1327112 | tf_op jit(solution)/shard_map/ppermute | solution.py:589
  7.5 0.0 collective-permute-start
  7.5 0.7 %collective-permute-start.1 = (f32[576,128]{1,0:T(8,128)S(1)}, f32[576,128]{1,0:T(8,128)S(1)}, u32[]{:S(2)}, u32[]{:S(2)}) collective-permute-start(f32[576,128]{1,0:T(8,128)S(1)} %get-tuple-element.30), channel_id=1, source_target_pairs={{1,2},{2,1},{3,4},{4,3},{5,6},{6,5},{9,10},{10,9},{11,12},{12,11},... | collective-permute-start | bytes 884744 | tf_op jit(solution)/shard_map/ppermute | solution.py:588
  8.2 0.7 %collective-permute-start.3 = (f32[480,128]{1,0:T(8,128)S(1)}, f32[480,128]{1,0:T(8,128)S(1)}, u32[]{:S(2)}, u32[]{:S(2)}) collective-permute-start(f32[480,128]{1,0:T(8,128)S(1)} %get-tuple-element.43), channel_id=1, source_target_pairs={{8,16},{16,8},{9,17},{17,9},{10,18},{18,10},{11,19},{19,11},{12,20... | collective-permute-start | bytes 737288 | tf_op jit(solution)/shard_map/ppermute | solution.py:590
  8.9 3.2 %shard_map.42 = (f32[82,160,128]{2,1,0:T(8,128)S(1)}, f32[82,160,128]{2,1,0:T(8,128)S(1)}, f32[82,160,128]{2,1,0:T(8,128)S(1)}, f32[82,160,128]{2,1,0:T(8,128)S(1)}) custom-call(f32[82,160,128]{2,1,0:T(8,128)S(1)} %get-tuple-element.25.field_in, f32[64,128]{1,0:T(8,128)S(1)} %get-tuple-element.26.stiff_ref), custom_call_target="tpu_custom_call", output_to_operand_aliasing={{0}: (0, {})} | custom-call | tf_op jit(solution)/shard_map/pallas_call | solution.py:279
  12.1 0.0 collective-permute-done.near
  12.1 0.0 collective-permute-done.1.far
  12.1 0.8 %shard_map.43 = (f32[82,160,128]{2,1,0:T(8,128)S(1)}, f32[82,160,128]{2,1,0:T(8,128)S(1)}, f32[160,128]{1,0:T(8,128)S(1)}, f32[544,128]{1,0:T(8,128)S(1)}) custom-call(f32[82,160,128]{2,1,0:T(8,128)S(1)} %get-tuple-element.27.field_in, f32[82,160,128]{2,1,0:T(8,128)S(1)} %get-tuple-element.28.stiff_in, ...), custom_call_target="tpu_custom_call", output_to_operand_aliasing={{0}: (0, {}), {1}: (1, {})} | custom-call | tf_op jit(solution)/shard_map/pallas_call | solution.py:175
  12.9 4.3 %collective-permute-start.4 = (f32[160,128]{1,0:T(8,128)S(1)}, f32[160,128]{1,0:T(8,128)S(1)}, u32[]{:S(2)}, u32[]{:S(2)}) collective-permute-start(f32[160,128]{1,0:T(8,128)S(1)} %get-tuple-element.44), channel_id=1, source_target_pairs={{0,8},{8,0},{16,24},{24,16},{1,9},{9,1},{17,25},{25,17},{2,10},{10... | collective-permute-start | bytes 245768 | tf_op jit(solution)/shard_map/ppermute | solution.py:593
  17.2 0.7 %collective-permute-start.5 = (f32[544,128]{1,0:T(8,128)S(1)}, f32[544,128]{1,0:T(8,128)S(1)}, u32[]{:S(2)}, u32[]{:S(2)}) collective-permute-start(f32[544,128]{1,0:T(8,128)S(1)} %get-tuple-element.45), channel_id=1, source_target_pairs={{8,16},{16,8},{9,17},{17,9},{10,18},{18,10},{11,19},{19,11},{12,20... | collective-permute-start | bytes 835592 | tf_op jit(solution)/shard_map/ppermute | solution.py:594
  17.9 0.6 %collective-permute-done.2.one = f32[864,128]{1,0:T(8,128)S(1)} collective-permute-done((f32[864,128]{1,0:T(8,128)S(1)}, f32[864,128]{1,0:T(8,128)S(1)}, u32[]{:S(2)}, u32[]{:S(2)}) %collective-permute-start.2) | collective-permute-done | bytes 442400 | tf_op jit(solution)/shard_map/ppermute | solution.py:589
  18.5 10.4 %shard_map.44 = (f32[82,160,128]{2,1,0:T(8,128)S(1)}, f32[82,160,128]{2,1,0:T(8,128)S(1)}, f32[82,160,128]{2,1,0:T(8,128)S(1)}, f32[82,160,128]{2,1,0:T(8,128)S(...) custom-call(f32[82,160,128]{2,1,0:T(8,128)S(1)} %get-tuple-element.3, ...), custom_call_target="tpu_custom_call", output_to_operand_aliasing={{0}: (0, {}), {1}: (1, {}), {2}: (2, {}), {3}: (3, {})} | custom-call | flops 10000000000 | bytes 41943040 | tf_op jit(solution)/shard_map/pallas_call | solution.py:349
  28.9 0.0 collective-permute-done.3.two
  28.9 0.0 collective-permute-done.4.corner_one
  28.9 0.0 collective-permute-done.5.whole
  28.9 5.6 %shard_map.45 = (f32[82,160,128]{2,1,0:T(8,128)S(1)}, f32[82,160,128]{2,1,0:T(8,128)S(1)}, f32[82,160,128]{2,1,0:T(8,128)S(1)}, f32[82,160,128]{2,1,0:T(8,128)S(...) custom-call(f32[82,160,128]{2,1,0:T(8,128)S(1)} %get-tuple-element.3, ...), custom_call_target="tpu_custom_call", output_to_operand_aliasing={{0}: (0, {}), {1}: (1, {}), {2}: (2, {}), {3}: (3, {}), {4}... | custom-call | tf_op jit(solution)/shard_map/pallas_call | solution.py:440
  34.5 1.7 %collective-permute-start.6 = (f32[96,128]{1,0:T(8,128)S(1)}, f32[96,128]{1,0:T(8,128)S(1)}, u32[]{:S(2)}, u32[]{:S(2)}) collective-permute-start(f32[96,128]{1,0:T(8,128)S(1)} %get-tuple-element.46), channel_id=1, source_target_pairs={{0,1},{1,0},{2,3},{3,2},{4,5},{5,4},{6,7},{7,6},{8,9},{9,8},{10,11... | collective-permute-start | bytes 147464 | tf_op jit(solution)/shard_map/ppermute | solution.py:578
  36.3 0.9 %collective-permute-done.6 = f32[96,128]{1,0:T(8,128)S(1)} collective-permute-done((f32[96,128]{1,0:T(8,128)S(1)}, f32[96,128]{1,0:T(8,128)S(1)}, u32[]{:S(2)}, u32[]{:S(2)}) %collective-permute-start.6) | collective-permute-done | bytes 49184 | tf_op jit(solution)/shard_map/ppermute | solution.py:578
  37.1 1.6 %collective-permute-start.7 = (f32[96,128]{1,0:T(8,128)S(1)}, f32[96,128]{1,0:T(8,128)S(1)}, u32[]{:S(2)}, u32[]{:S(2)}) collective-permute-start(f32[96,128]{1,0:T(8,128)S(1)} %add.15), channel_id=1, source_target_pairs={{0,2},{1,3},{2,0},{3,1},{4,6},{5,7},{6,4},{7,5},{8,10},{9,11},{10,... | collective-permute-start | bytes 147464 | tf_op jit(solution)/shard_map/ppermute | solution.py:578
  38.7 2.5 %collective-permute-done.7 = f32[96,128]{1,0:T(8,128)S(1)} collective-permute-done((f32[96,128]{1,0:T(8,128)S(1)}, f32[96,128]{1,0:T(8,128)S(1)}, u32[]{:S(2)}, u32[]{:S(2)}) %collective-permute-start.7) | collective-permute-done | bytes 49184 | tf_op jit(solution)/shard_map/ppermute | solution.py:578
  41.2 2.6 %collective-permute-start.8 = (f32[96,128]{1,0:T(8,128)S(1)}, f32[96,128]{1,0:T(8,128)S(1)}, u32[]{:S(2)}, u32[]{:S(2)}) collective-permute-start(f32[96,128]{1,0:T(8,128)S(1)} %add.16), channel_id=1, source_target_pairs={{0,4},{1,5},{2,6},{3,7},{4,0},{5,1},{6,2},{7,3},{8,12},{9,13},{10,... | collective-permute-start | bytes 147464 | tf_op jit(solution)/shard_map/ppermute | solution.py:578
  43.9 2.4 %collective-permute-done.8 = f32[96,128]{1,0:T(8,128)S(1)} collective-permute-done((f32[96,128]{1,0:T(8,128)S(1)}, f32[96,128]{1,0:T(8,128)S(1)}, u32[]{:S(2)}, u32[]{:S(2)}) %collective-permute-start.8) | collective-permute-done | bytes 49184 | tf_op jit(solution)/shard_map/ppermute | solution.py:578
  46.3 3.1 %collective-permute-start.9 = (f32[96,128]{1,0:T(8,128)S(1)}, f32[96,128]{1,0:T(8,128)S(1)}, u32[]{:S(2)}, u32[]{:S(2)}) collective-permute-start(f32[96,128]{1,0:T(8,128)S(1)} %add.17), channel_id=1, source_target_pairs={{0,8},{1,9},{2,10},{3,11},{4,12},{5,13},{6,14},{7,15},{8,0},{9,1},... | collective-permute-start | bytes 147464 | tf_op jit(solution)/shard_map/ppermute | solution.py:578
  49.4 2.1 %collective-permute-done.9 = f32[96,128]{1,0:T(8,128)S(1)} collective-permute-done((f32[96,128]{1,0:T(8,128)S(1)}, f32[96,128]{1,0:T(8,128)S(1)}, u32[]{:S(2)}, u32[]{:S(2)}) %collective-permute-start.9) | collective-permute-done | bytes 49184 | tf_op jit(solution)/shard_map/ppermute | solution.py:578
  51.5 1.6 %collective-permute-start.10 = (f32[96,128]{1,0:T(8,128)S(1)}, f32[96,128]{1,0:T(8,128)S(1)}, u32[]{:S(2)}, u32[]{:S(2)}) collective-permute-start(f32[96,128]{1,0:T(8,128)S(1)} %add.18), channel_id=1, source_target_pairs={{0,16},{1,17},{2,18},{3,19},{4,20},{5,21},{6,22},{7,23},{8,24},{9,... | collective-permute-start | bytes 147464 | tf_op jit(solution)/shard_map/ppermute | solution.py:578
  53.1 2.5 %collective-permute-done.10 = f32[96,128]{1,0:T(8,128)S(1)} collective-permute-done((f32[96,128]{1,0:T(8,128)S(1)}, f32[96,128]{1,0:T(8,128)S(1)}, u32[]{:S(2)}, u32[]{:S(2)}) %collective-permute-start.10) | collective-permute-done | bytes 49184 | tf_op jit(solution)/shard_map/ppermute | solution.py:578
  55.6 7.1 %shard_map.46 = (f32[96,64,128]{2,1,0:T(8,128)}, f32[96,96]{1,0:T(8,128)}) custom-call(f32[96,128]{1,0:T(8,128)S(1)} %add.19.sums_ref, f32[64,96,128]{2,1,0:T(8,128)S(1)} %get-tuple-element.47.turned), custom_call_target="tpu_custom_call" | custom-call | tf_op jit(solution)/shard_map/pallas_call | solution.py:547
  (5 shorter events, 0.0 us)
Async XLA Ops:
  4.5 14.0 %collective-permute-start.2 = (f32[864,128]{1,0:T(8,128)S(1)}, f32[864,128]{1,0:T(8,128)S(1)}, u32[]{:S(2)}, u32[]{:S(2)}) collective-permute-start(f32[864,128]{1,0:T(8,128)S(1)} %get-tuple-element.36), channel_id=1, source_target_pairs={{0,8},{8,0},{16,24},{24,16},{1,9},{9,1},{17,25},{25,17},{2,10},{10... | collective-permute-start | bytes 1327112 | tf_op jit(solution)/shard_map/ppermute | solution.py:589
  7.5 4.6 %collective-permute-start = (f32[576,128]{1,0:T(8,128)S(1)}, f32[576,128]{1,0:T(8,128)S(1)}, u32[]{:S(2)}, u32[]{:S(2)}) collective-permute-start(f32[576,128]{1,0:T(8,128)S(1)} %get-tuple-element.29), channel_id=1, source_target_pairs={{0,1},{1,0},{2,3},{3,2},{4,5},{5,4},{6,7},{7,6},{8,9},{9,8},{10,11... | collective-permute-start | bytes 884744 | tf_op jit(solution)/shard_map/ppermute | solution.py:587
  7.5 4.6 %collective-permute-start.1 = (f32[576,128]{1,0:T(8,128)S(1)}, f32[576,128]{1,0:T(8,128)S(1)}, u32[]{:S(2)}, u32[]{:S(2)}) collective-permute-start(f32[576,128]{1,0:T(8,128)S(1)} %get-tuple-element.30), channel_id=1, source_target_pairs={{1,2},{2,1},{3,4},{4,3},{5,6},{6,5},{9,10},{10,9},{11,12},{12,11},... | collective-permute-start | bytes 884744 | tf_op jit(solution)/shard_map/ppermute | solution.py:588
  8.2 20.7 %collective-permute-start.3 = (f32[480,128]{1,0:T(8,128)S(1)}, f32[480,128]{1,0:T(8,128)S(1)}, u32[]{:S(2)}, u32[]{:S(2)}) collective-permute-start(f32[480,128]{1,0:T(8,128)S(1)} %get-tuple-element.43), channel_id=1, source_target_pairs={{8,16},{16,8},{9,17},{17,9},{10,18},{18,10},{11,19},{19,11},{12,20... | collective-permute-start | bytes 737288 | tf_op jit(solution)/shard_map/ppermute | solution.py:590
  12.9 16.0 %collective-permute-start.4 = (f32[160,128]{1,0:T(8,128)S(1)}, f32[160,128]{1,0:T(8,128)S(1)}, u32[]{:S(2)}, u32[]{:S(2)}) collective-permute-start(f32[160,128]{1,0:T(8,128)S(1)} %get-tuple-element.44), channel_id=1, source_target_pairs={{0,8},{8,0},{16,24},{24,16},{1,9},{9,1},{17,25},{25,17},{2,10},{10... | collective-permute-start | bytes 245768 | tf_op jit(solution)/shard_map/ppermute | solution.py:593
  17.2 11.7 %collective-permute-start.5 = (f32[544,128]{1,0:T(8,128)S(1)}, f32[544,128]{1,0:T(8,128)S(1)}, u32[]{:S(2)}, u32[]{:S(2)}) collective-permute-start(f32[544,128]{1,0:T(8,128)S(1)} %get-tuple-element.45), channel_id=1, source_target_pairs={{8,16},{16,8},{9,17},{17,9},{10,18},{18,10},{11,19},{19,11},{12,20... | collective-permute-start | bytes 835592 | tf_op jit(solution)/shard_map/ppermute | solution.py:594
  34.5 2.6 %collective-permute-start.6 = (f32[96,128]{1,0:T(8,128)S(1)}, f32[96,128]{1,0:T(8,128)S(1)}, u32[]{:S(2)}, u32[]{:S(2)}) collective-permute-start(f32[96,128]{1,0:T(8,128)S(1)} %get-tuple-element.46), channel_id=1, source_target_pairs={{0,1},{1,0},{2,3},{3,2},{4,5},{5,4},{6,7},{7,6},{8,9},{9,8},{10,11... | collective-permute-start | bytes 147464 | tf_op jit(solution)/shard_map/ppermute | solution.py:578
  37.1 4.1 %collective-permute-start.7 = (f32[96,128]{1,0:T(8,128)S(1)}, f32[96,128]{1,0:T(8,128)S(1)}, u32[]{:S(2)}, u32[]{:S(2)}) collective-permute-start(f32[96,128]{1,0:T(8,128)S(1)} %add.15), channel_id=1, source_target_pairs={{0,2},{1,3},{2,0},{3,1},{4,6},{5,7},{6,4},{7,5},{8,10},{9,11},{10,... | collective-permute-start | bytes 147464 | tf_op jit(solution)/shard_map/ppermute | solution.py:578
  41.2 5.0 %collective-permute-start.8 = (f32[96,128]{1,0:T(8,128)S(1)}, f32[96,128]{1,0:T(8,128)S(1)}, u32[]{:S(2)}, u32[]{:S(2)}) collective-permute-start(f32[96,128]{1,0:T(8,128)S(1)} %add.16), channel_id=1, source_target_pairs={{0,4},{1,5},{2,6},{3,7},{4,0},{5,1},{6,2},{7,3},{8,12},{9,13},{10,... | collective-permute-start | bytes 147464 | tf_op jit(solution)/shard_map/ppermute | solution.py:578
  46.3 5.2 %collective-permute-start.9 = (f32[96,128]{1,0:T(8,128)S(1)}, f32[96,128]{1,0:T(8,128)S(1)}, u32[]{:S(2)}, u32[]{:S(2)}) collective-permute-start(f32[96,128]{1,0:T(8,128)S(1)} %add.17), channel_id=1, source_target_pairs={{0,8},{1,9},{2,10},{3,11},{4,12},{5,13},{6,14},{7,15},{8,0},{9,1},... | collective-permute-start | bytes 147464 | tf_op jit(solution)/shard_map/ppermute | solution.py:578
  51.5 4.2 %collective-permute-start.10 = (f32[96,128]{1,0:T(8,128)S(1)}, f32[96,128]{1,0:T(8,128)S(1)}, u32[]{:S(2)}, u32[]{:S(2)}) collective-permute-start(f32[96,128]{1,0:T(8,128)S(1)} %add.18), channel_id=1, source_target_pairs={{0,16},{1,17},{2,18},{3,19},{4,20},{5,21},{6,22},{7,23},{8,24},{9,... | collective-permute-start | bytes 147464 | tf_op jit(solution)/shard_map/ppermute | solution.py:578

commit v2 on v1

--- a/solution.py
+++ b/solution.py
@@ -16,7 +16,7 @@
 HALO = 2 * DEGREE + 1
 MARGIN = HALO - 1
 FIRST = 5
-EARLY = 1
+EARLY = 2
 LANES = 128
 PAD = 16
 GROUP = 4
@@ -136,6 +136,8 @@
 def corner_kernel(vectors, field_in, stiff_in, stiff_ref, near, far, rest, field, stiff, one, whole):
     rows, cols = stiff_ref.shape
     col_first, row_first = even(lax.axis_index("col")), even(lax.axis_index("row"))
+    left = jnp.where(lax.axis_index("col") == 0, 0.0, 1.0)
+    right = jnp.where(lax.axis_index("col") == lax.axis_size("col") - 1, 0.0, 1.0)
     step = 8
     ends = (PAD - MARGIN, PAD + cols)
 
@@ -143,8 +145,8 @@
         for r in range(step):
             x = i * step + r
             a, b = near[pl.ds(x * HALO, HALO), :], far[pl.ds(x * HALO, HALO), :]
-            field[HALO + x, PAD - HALO : PAD, :] = jnp.where(col_first, b, a)
-            field[HALO + x, PAD + cols : PAD + cols + HALO, :] = jnp.where(col_first, a, b)
+            field[HALO + x, PAD - HALO : PAD, :] = jnp.where(col_first, b, a) * left
+            field[HALO + x, PAD + cols : PAD + cols + HALO, :] = jnp.where(col_first, a, b) * right
         for r in range(step):
             x = HALO + i * step + r
             for y in ends:
@@ -226,11 +228,11 @@
             work(x, y, min(step, high - x))
 
 
-def clear_cols(field, low, high, cols):
+def clear_cols(field, low, height, cols):
     col, count = lax.axis_index("col"), lax.axis_size("col")
 
     def at(start):
-        field[low:high, start : start + MARGIN, :] = jnp.zeros((high - low, MARGIN, LANES), F32)
+        field[pl.ds(low, height), start : start + MARGIN, :] = jnp.zeros((height, MARGIN, LANES), F32)
 
     pl.when(col == 0)(lambda: at(PAD - MARGIN))
     pl.when(col == count - 1)(lambda: at(PAD + cols))
@@ -295,11 +297,12 @@
 
 
 def multiply(slot, xs, cols, field, inner, lhs, sums):
+    width = len(xs) * cols
     for which, ref in enumerate((field, inner)):
         cells = jnp.concatenate([ref[HALO + x, PAD : PAD + cols, :] for x in xs], axis=0)
         high, low = split(cells)
         sums[which] += jnp.dot(
-            lhs[slot, which], jnp.concatenate([high, low], axis=1), preferred_element_type=F32
+            lhs[slot, which, :, :width], jnp.concatenate([high, low], axis=1), preferred_element_type=F32
         )
 
 
@@ -316,7 +319,7 @@
             bends = [y for y in tiles if y not in tiles_of(cols, 2 * k + 2)]
             advances = [y for y in tiles if y not in tiles_of(cols, 2 * k + 3)]
         operator(k, rows, bends, advances, field, odd, inner, stiff)
-        clear_cols(terms[(k + 1) % 2], HALO + 2 + 2 * k, HALO + rows - 2 - 2 * k, cols)
+        clear_cols(terms[(k + 1) % 2], HALO + 2 + 2 * k, rows - 4 - 4 * k, cols)
     low, high = HALO, rows - HALO
     own = range(PAD, PAD + cols, 8)
     sweep(HALO + low, HALO + high, own, functools.partial(root_bend, terms[DEGREE % 2], stiff, inner))
@@ -365,62 +368,66 @@
     )(field, odd, inner, stiff, one)
 
 
-def ends_kernel(vectors, rows, cols, field_in, odd_in, inner_in, stiff_in, turned_in, sums_in,
-                two, corner_one, whole, field, odd, inner, stiff, turned, packed, sums, lhs):
+def end_kernel(vectors, rows, cols, last, field_in, odd_in, inner_in, stiff_in, turned_in, sums_in,
+               *refs):
+    if last:
+        two, corner, field, odd, inner, stiff, turned, packed, sums, lhs = refs
+        corner_at = (HALO - FIRST) * vectors
+    else:
+        corner, field, odd, inner, stiff, turned, sums, lhs = refs
+        corner_at = 0
     row_first = even(lax.axis_index("row"))
-    base = 2 * HALO * MARGIN
-
-    def fill(start, row_block, corner):
-        for r in range(HALO):
-            x = start + r
-            weight = corner[base + r : base + r + 1, :]
-            if row_block is not None:
-                field[x, PAD : PAD + cols, :] = lanes_up(row_block(r), weight)
-            stiff[x, PAD : PAD + cols, :] = spread_stiffness(weight)
-            for e, y in enumerate((PAD - MARGIN, PAD + cols)):
-                piece = corner[(2 * r + e) * MARGIN : (2 * r + e + 1) * MARGIN, :]
-                field[x, y : y + MARGIN, :] = piece
-                stiff[x, y : y + MARGIN, :] = jnp.broadcast_to(
-                    piece[:, vectors : vectors + 1] * (2.0 / HALF), (MARGIN, LANES)
-                )
-
-    def second(r):
-        ref, at = (two, r) if r < FIRST else (whole, r - FIRST)
-        return ref[at * vectors : (at + 1) * vectors, :]
-
-    fill(jnp.where(row_first, HALO + rows, 0), None, corner_one)
-    fill(jnp.where(row_first, 0, HALO + rows), second, whole.at[(HALO - FIRST) * vectors :, :])
-
-    def both(low, high, ys, work):
-        flip = rows + 2 * HALO
-
-        def side(i):
-            x = low + i * (flip - high - low)
-            for y in ys:
-                work(x, y, 4)
-                work(x + 4, y, high - low - 4)
-
-        loop(2, side)
+    side = jnp.where(row_first, 0 if last else 1, 1 if last else 0)
+    base = corner_at + 2 * HALO * MARGIN
+    start = side * (HALO + rows)
+    for r in range(HALO):
+        x = start + r
+        weight = corner[base + r : base + r + 1, :]
+        if last:
+            ref, at = (two, r) if r < FIRST else (corner, r - FIRST)
+            block = ref[at * vectors : (at + 1) * vectors, :]
+            field[x, PAD : PAD + cols, :] = lanes_up(block, weight)
+        stiff[x, PAD : PAD + cols, :] = spread_stiffness(weight)
+        for e, y in enumerate((PAD - MARGIN, PAD + cols)):
+            at = corner_at + (2 * r + e) * MARGIN
+            piece = corner[at : at + MARGIN, :]
+            field[x, y : y + MARGIN, :] = piece
+            stiff[x, y : y + MARGIN, :] = jnp.broadcast_to(
+                piece[:, vectors : vectors + 1] * (2.0 / HALF), (MARGIN, LANES)
+            )
+    if last:
+        clear_rows(field, rows, cols)
+        clear_rows(stiff, rows, cols)
+
+    def some_rows(low, ys, work):
+        x = low + side * (rows + HALO - 2 * low)
+        for y in ys:
+            work(x, y, 4)
+            work(x + 4, y, HALO - 4)
 
     terms = (field, odd)
     for k in range(DEGREE):
         current, following = terms[k % 2], terms[(k + 1) % 2]
         low = 1 + 2 * k
         tiles = tiles_of(cols, 0)
-        both(low, low + HALO, tiles, functools.partial(bend, current, stiff, inner))
-        both(low + 1, low + 1 + HALO, tiles, functools.partial(advance, k, current, inner, following))
-        clear_cols(following, low + 1, low + 1 + HALO, cols)
-        clear_cols(following, rows + 2 * HALO - low - 1 - HALO, rows + 2 * HALO - low - 1, cols)
-        clear_rows(following, rows, cols)
+        some_rows(low, tiles, functools.partial(bend, current, stiff, inner))
+        some_rows(low + 1, tiles, functools.partial(advance, k, current, inner, following))
+        clear_cols(following, low + 1 + side * (rows + HALO - 2 * low - 2), HALO, cols)
+        if last:
+            clear_rows(following, rows, cols)
     final = terms[DEGREE % 2]
-    both(HALO, 2 * HALO, tiles_of(cols, 1), functools.partial(root_bend, final, stiff, inner))
-
-    sums[...] = sums_in[...]
-    xs = list(range(HALO + 1)) + list(range(rows - HALO - 1, rows))
-    for g in range(0, len(xs), GROUP):
-        for j, x in enumerate(xs[g : g + GROUP]):
+    some_rows(HALO, tiles_of(cols, 1), functools.partial(root_bend, final, stiff, inner))
+
+    if last:
+        sums[...] = sums_in[...]
+    first = side * (rows - HALO - 1)
+    for g in range(0, HALO + 1, GROUP):
+        xs = [first + x for x in range(g, min(g + GROUP, HALO + 1))]
+        for j, x in enumerate(xs):
             prepare(g // GROUP % 2, x, j, vectors, cols, final, inner, turned, lhs)
-        multiply(g // GROUP % 2, xs[g : g + GROUP], cols, final, inner, lhs, sums)
+        multiply(g // GROUP % 2, xs, cols, final, inner, lhs, sums)
+    if not last:
+        return
 
     def total(which):
         high, low = sums[which, :, :LANES], sums[which, :, LANES:]
@@ -435,27 +442,22 @@
     packed[...] = jnp.where(j < vectors, both_grams, jnp.where(j == vectors, diagonal, 0.0))
 
 
-def ends(vectors, rows, cols, field, odd, inner, stiff, turned, sums, two, corner_one, whole):
+def end(vectors, rows, cols, state, halo):
+    last = len(halo) > 1
     big = padded(rows, cols)
+    shapes = [big] * 4 + [jax.ShapeDtypeStruct((rows, vectors, cols), F32)]
+    sums = (2, vectors, 2 * LANES)
+    shapes.append(jax.ShapeDtypeStruct((vectors, LANES) if last else sums, F32))
     return pl.pallas_call(
-        functools.partial(ends_kernel, vectors, rows, cols),
-        in_specs=[VMEM] * 9,
+        functools.partial(end_kernel, vectors, rows, cols, last),
+        in_specs=[VMEM] * (6 + len(halo)),
         out_specs=[VMEM] * 6,
-        out_shape=[
-            big,
-            big,
-            big,
-            big,
-            jax.ShapeDtypeStruct((rows, vectors, cols), F32),
-            jax.ShapeDtypeStruct((vectors, LANES), F32),
-        ],
-        input_output_aliases={0: 0, 1: 1, 2: 2, 3: 3, 4: 4},
-        scratch_shapes=[
-            pltpu.VMEM((2, vectors, 2 * LANES), F32),
-            pltpu.VMEM((2, 2, vectors, GROUP * cols), BF16),
-        ],
+        out_shape=shapes,
+        input_output_aliases={i: i for i in range(5 if last else 6)},
+        scratch_shapes=([pltpu.VMEM(sums, F32)] if last else [])
+        + [pltpu.VMEM((2, 2, vectors, GROUP * cols), BF16)],
         compiler_params=params(8),
-    )(field, odd, inner, stiff, turned, sums, two, corner_one, whole)[4:]
+    )(*state, *halo)
 
 
 def inverse_factor(gram, vectors):
@@ -562,8 +564,18 @@
 
 def pairs(count, start):
     found = []
-    for i in range(start, count - 1, 2):
-        found += [(i, i + 1), (i + 1, i)]
+    for i in range(start, start + count - 1, 2):
+        found += [(i % count, (i + 1) % count), ((i + 1) % count, i % count)]
+    return found
+
+
+def inner_pairs(row_count, col_count):
+    found = []
+    for r in range(row_count):
+        for c in range(col_count):
+            beside = c + 1 if c % 2 else c - 1
+            there = (r, beside) if 0 <= beside < col_count else (r ^ (row_count // 2), c)
+            found.append((r * col_count + c, there[0] * col_count + there[1]))
     return found
 
 
@@ -575,7 +587,7 @@
         return lax.psum(values, axes)
     step = 1
     while step < count:
-        values = values + lax.ppermute(values, axes, [(i, i ^ step) for i in range(count)])
+        values = values + lax.ppermute(values, axes, [(i, i ^ (step | 1)) for i in range(count)])
         step *= 2
     return values
 
@@ -585,15 +597,16 @@
     row_count, col_count = lax.axis_size("row"), lax.axis_size("col")
     field, near, far, one, two, rest, stiffness = turn(start_block, stiffness)
     near = lax.ppermute(near, "col", pairs(col_count, 0))
-    far = lax.ppermute(far, "col", pairs(col_count, 1))
+    far = lax.ppermute(far, ("row", "col"), inner_pairs(row_count, col_count))
     one = lax.ppermute(one, "row", pairs(row_count, 0))
     two = lax.ppermute(two, "row", pairs(row_count, 1))
     field, stiff, odd, inner = early(field, stiffness)
     field, stiff, corner_one, whole = corners(vectors, field, stiff, stiffness, near, far, rest)
     corner_one = lax.ppermute(corner_one, "row", pairs(row_count, 0))
     whole = lax.ppermute(whole, "row", pairs(row_count, 1))
-    field, odd, inner, stiff, turned, sums = middle(vectors, rows, cols, field, odd, inner, stiff, one)
-    turned, sums = ends(vectors, rows, cols, field, odd, inner, stiff, turned, sums, two, corner_one, whole)
+    state = middle(vectors, rows, cols, field, odd, inner, stiff, one)
+    state = end(vectors, rows, cols, state, (corner_one,))
+    *_, turned, sums = end(vectors, rows, cols, state, (two, whole))
     sums = all_sum(sums, ("row", "col"))
     scale = float(rows * row_count * cols * col_count) ** 0.5
     return tuple(finish(sums, turned, scale))

time: 63.1 us -> 60.4 us (0.957)
  starting transfers between devices: 20 us -> 13.1 us
  waiting for transfers between devices: 11 us -> 14.3 us
  Pallas kernels: 30.9 us -> 31.8 us
    ppermute x6, starting transfers between devices: 11.4 us -> 6.93 us  [the longest x5 5.42 us: all_sum(): lax.ppermute(values, axes, [(i, i ^ (step | 1)) for i in range(count)])]
    ppermute x1, starting transfers between devices: 4.28 us -> 1.12 us  [body(): corner_one = lax.ppermute(corner_one, 'row', pairs(row_count, 0))]
    ppermute x6, waiting for transfers between devices: 10.4 us -> 12.8 us  [the longest x5 12 us: all_sum(): lax.ppermute(values, axes, [(i, i ^ (step | 1)) for i in range(count)])]
    ppermute x1, starting transfers between devices: 0.67 us -> 1.92 us  [body(): whole = lax.ppermute(whole, 'row', pairs(row_count, 1))]
    ppermute x1, waiting for transfers between devices: 0.01 us -> 1.1 us  [body(): whole = lax.ppermute(whole, 'row', pairs(row_count, 1))]
    pallas_call x1, Pallas kernels: 3.2 us -> 4.25 us  [early(): pl.pallas_call(early_kernel, in_specs=[VMEM] * 2, out_specs=[VMEM] * 4, o...]
    pallas_call x1, Pallas kernels: 10.4 us -> 9.41 us  [middle(): pl.pallas_call(functools.partial(middle_kernel, vectors, rows, cols), in_...]
    pallas_call x1 -> x2, Pallas kernels: 5.59 us -> 6.36 us  [end(): pl.pallas_call(functools.partial(end_kernel, vectors, rows, cols, last),...]
  transfers between devices with their start and end apart: 11 -> 11, of which waited for: 6 -> 8; matrix products, arithmetic and copies ran while one was open for 0% -> 0% of each run, Pallas kernels for 23% -> 29%
where the time goes in v2:
time: 60.4 us; the launch traced here: 60.1 us
  Pallas kernels  31.8 us (53%)
  waiting for transfers between devices  14.3 us (24%)
  starting transfers between devices  13.1 us (22%)
  between operations  0.87 us (1%)
    ppermute x5, waiting for transfers between devices, all_sum(): lax.ppermute(values, axes, [(i, i ^ (step | 1)) for i in range(count)])  12 us
    pallas_call x1, Pallas kernels, middle(): pl.pallas_call(functools.partial(middle_kernel, vectors, rows, cols), in_...  9.41 us
    pallas_call x1, Pallas kernels, finish(): pl.pallas_call(functools.partial(finish_kernel, scale), in_specs=[VMEM, V...  7.11 us
    pallas_call x2, Pallas kernels, end(): pl.pallas_call(functools.partial(end_kernel, vectors, rows, cols, last),...  6.36 us
    ppermute x5, starting transfers between devices, all_sum(): lax.ppermute(values, axes, [(i, i ^ (step | 1)) for i in range(count)])  5.42 us
    pallas_call x1, Pallas kernels, early(): pl.pallas_call(early_kernel, in_specs=[VMEM] * 2, out_specs=[VMEM] * 4, o...  4.25 us
    pallas_call x1, Pallas kernels, turn(): pl.pallas_call(turn_kernel, in_specs=[HBM] * 2, out_specs=[VMEM] * 7, out...  3.89 us
    ppermute x1, starting transfers between devices, body(): one = lax.ppermute(one, 'row', pairs(row_count, 0))  3 us
  transfers between devices with their start and end apart: 11, of which 8 were waited for; matrix products, arithmetic and copies ran while one was open for 0% of the time, Pallas kernels for 29%

profile of v2, /device:TPU:0, one launch (start us, length us, event | category | flops | bytes accessed | tf_op | source)
XLA Modules:
  0.0 60.1 jit_solution(13157457599922210489)
XLA Ops:
  0.6 3.9 %shard_map.41 = (f32[82,160,128]{2,1,0:T(8,128)S(1)}, f32[576,128]{1,0:T(8,128)S(1)}, f32[576,128]{1,0:T(8,128)S(1)}, f32[864,128]{1,0:T(8,128)S(1)}, f32[480,12...) custom-call(f32[96,64,128]{2,1,0:T(8,128)} %block_ref.1, f32[64,128]{1,0:T(8,128)} %stiff_ref.1), custom_call_target="tpu_custom_call" | custom-call | bytes 6291456 | tf_op jit(solution)/shard_map/pallas_call | solution.py:110
  4.5 3.0 %collective-permute-start.2 = (f32[864,128]{1,0:T(8,128)S(1)}, f32[864,128]{1,0:T(8,128)S(1)}, u32[]{:S(2)}, u32[]{:S(2)}) collective-permute-start(f32[864,128]{1,0:T(8,128)S(1)} %get-tuple-element.42), channel_id=1, source_target_pairs={{0,8},{8,0},{16,24},{24,16},{1,9},{9,1},{17,25},{25,17},{2,10},{10... | collective-permute-start | bytes 1327112 | tf_op jit(solution)/shard_map/ppermute | solution.py:601
  7.5 0.0 collective-permute-start
  7.5 1.5 %collective-permute-start.1 = (f32[576,128]{1,0:T(8,128)S(1)}, f32[576,128]{1,0:T(8,128)S(1)}, u32[]{:S(2)}, u32[]{:S(2)}) collective-permute-start(f32[576,128]{1,0:T(8,128)S(1)} %get-tuple-element.36), channel_id=1, source_target_pairs={{0,16},{1,2},{2,1},{3,4},{4,3},{5,6},{6,5},{7,23},{8,24},{9,10},{1... | collective-permute-start | bytes 884744 | tf_op jit(solution)/shard_map/ppermute | solution.py:600
  9.1 0.1 collective-permute-start.4
  9.1 4.2 %shard_map.42 = (f32[82,160,128]{2,1,0:T(8,128)S(1)}, f32[82,160,128]{2,1,0:T(8,128)S(1)}, f32[82,160,128]{2,1,0:T(8,128)S(1)}, f32[82,160,128]{2,1,0:T(8,128)S(1)}) custom-call(f32[82,160,128]{2,1,0:T(8,128)S(1)} %get-tuple-element.31.field_in, f32[64,128]{1,0:T(8,128)S(1)} %get-tuple-element.32.stiff_ref), custom_call_target="tpu_custom_call", output_to_operand_aliasing={{0}: (0, {})} | custom-call | tf_op jit(solution)/shard_map/pallas_call | solution.py:281
  13.4 0.0 collective-permute-done.near
  13.4 0.8 %collective-permute-done.1.far = f32[576,128]{1,0:T(8,128)S(1)} collective-permute-done((f32[576,128]{1,0:T(8,128)S(1)}, f32[576,128]{1,0:T(8,128)S(1)}, u32[]{:S(2)}, u32[]{:S(2)}) %collective-permute-start.1) | collective-permute-done | bytes 294944 | tf_op jit(solution)/shard_map/ppermute | solution.py:600
  14.3 0.8 %shard_map.43 = (f32[82,160,128]{2,1,0:T(8,128)S(1)}, f32[82,160,128]{2,1,0:T(8,128)S(1)}, f32[160,128]{1,0:T(8,128)S(1)}, f32[544,128]{1,0:T(8,128)S(1)}) custom-call(f32[82,160,128]{2,1,0:T(8,128)S(1)} %get-tuple-element.33.field_in, f32[82,160,128]{2,1,0:T(8,128)S(1)} %get-tuple-element.34.stiff_in, ...), custom_call_target="tpu_custom_call", output_to_operand_aliasing={{0}: (0, {}), {1}: (1, {})} | custom-call | tf_op jit(solution)/shard_map/pallas_call | solution.py:177
  15.1 1.1 %collective-permute-start.3 = (f32[160,128]{1,0:T(8,128)S(1)}, f32[160,128]{1,0:T(8,128)S(1)}, u32[]{:S(2)}, u32[]{:S(2)}) collective-permute-start(f32[160,128]{1,0:T(8,128)S(1)} %get-tuple-element.49), channel_id=1, source_target_pairs={{0,8},{8,0},{16,24},{24,16},{1,9},{9,1},{17,25},{25,17},{2,10},{10... | collective-permute-start | bytes 245768 | tf_op jit(solution)/shard_map/ppermute | solution.py:605
  16.2 1.9 %collective-permute-start.5 = (f32[544,128]{1,0:T(8,128)S(1)}, f32[544,128]{1,0:T(8,128)S(1)}, u32[]{:S(2)}, u32[]{:S(2)}) collective-permute-start(f32[544,128]{1,0:T(8,128)S(1)} %get-tuple-element.57), channel_id=1, source_target_pairs={{8,16},{16,8},{24,0},{0,24},{9,17},{17,9},{25,1},{1,25},{10,18},{1... | collective-permute-start | bytes 835592 | tf_op jit(solution)/shard_map/ppermute | solution.py:606
  18.1 0.4 collective-permute-done.2.one
  18.5 9.4 %shard_map.44 = (f32[82,160,128]{2,1,0:T(8,128)S(1)}, f32[82,160,128]{2,1,0:T(8,128)S(1)}, f32[82,160,128]{2,1,0:T(8,128)S(1)}, f32[82,160,128]{2,1,0:T(8,128)S(...) custom-call(f32[82,160,128]{2,1,0:T(8,128)S(1)} %get-tuple-element.3, ...), custom_call_target="tpu_custom_call", output_to_operand_aliasing={{0}: (0, {}), {1}: (1, {}), {2}: (2, {}), {3}: (3, {})} | custom-call | flops 10000000000 | bytes 41943040 | tf_op jit(solution)/shard_map/pallas_call | solution.py:352
  27.9 0.0 collective-permute-done.3.refs_0_
  27.9 2.8 %shard_map.45 = (f32[82,160,128]{2,1,0:T(8,128)S(1)}, f32[82,160,128]{2,1,0:T(8,128)S(1)}, f32[82,160,128]{2,1,0:T(8,128)S(1)}, f32[82,160,128]{2,1,0:T(8,128)S(...) custom-call(f32[82,160,128]{2,1,0:T(8,128)S(1)} %get-tuple-element.4, ...), custom_call_target="tpu_custom_call", output_to_operand_aliasing={{0}: (0, {}), {1}: (1, {}), {2}: (2, {}), {3}: (3, {}), {4}... | custom-call | tf_op jit(solution)/shard_map/pallas_call | solution.py:451
  30.8 0.0 collective-permute-done.4.refs_0_
  30.8 1.1 %collective-permute-done.5.refs_1_ = f32[544,128]{1,0:T(8,128)S(1)} collective-permute-done((f32[544,128]{1,0:T(8,128)S(1)}, f32[544,128]{1,0:T(8,128)S(1)}, u32[]{:S(2)}, u32[]{:S(2)}) %collective-permute-start.5) | collective-permute-done | bytes 278560 | tf_op jit(solution)/shard_map/ppermute | solution.py:606
  31.9 3.5 %shard_map.46 = (f32[82,160,128]{2,1,0:T(8,128)S(1)}, f32[82,160,128]{2,1,0:T(8,128)S(1)}, f32[82,160,128]{2,1,0:T(8,128)S(1)}, f32[82,160,128]{2,1,0:T(8,128)S(...) custom-call(f32[82,160,128]{2,1,0:T(8,128)S(1)} %get-tuple-element.5, ...), custom_call_target="tpu_custom_call", output_to_operand_aliasing={{0}: (0, {}), {1}: (1, {}), {2}: (2, {}), {3}: (3, {}), {4}... | custom-call | tf_op jit(solution)/shard_map/pallas_call | solution.py:451
  35.4 0.1 collective-permute-start.6
  35.5 1.2 %collective-permute-done.6 = f32[96,128]{1,0:T(8,128)S(1)} collective-permute-done((f32[96,128]{1,0:T(8,128)S(1)}, f32[96,128]{1,0:T(8,128)S(1)}, u32[]{:S(2)}, u32[]{:S(2)}) %collective-permute-start.6) | collective-permute-done | bytes 49184 | tf_op jit(solution)/shard_map/ppermute | solution.py:590
  36.7 1.3 %collective-permute-start.7 = (f32[96,128]{1,0:T(8,128)S(1)}, f32[96,128]{1,0:T(8,128)S(1)}, u32[]{:S(2)}, u32[]{:S(2)}) collective-permute-start(f32[96,128]{1,0:T(8,128)S(1)} %add.15), channel_id=1, source_target_pairs={{0,3},{1,2},{2,1},{3,0},{4,7},{5,6},{6,5},{7,4},{8,11},{9,10},{10,... | collective-permute-start | bytes 147464 | tf_op jit(solution)/shard_map/ppermute | solution.py:590
  38.1 2.5 %collective-permute-done.7 = f32[96,128]{1,0:T(8,128)S(1)} collective-permute-done((f32[96,128]{1,0:T(8,128)S(1)}, f32[96,128]{1,0:T(8,128)S(1)}, u32[]{:S(2)}, u32[]{:S(2)}) %collective-permute-start.7) | collective-permute-done | bytes 49184 | tf_op jit(solution)/shard_map/ppermute | solution.py:590
  40.6 2.4 %collective-permute-start.8 = (f32[96,128]{1,0:T(8,128)S(1)}, f32[96,128]{1,0:T(8,128)S(1)}, u32[]{:S(2)}, u32[]{:S(2)}) collective-permute-start(f32[96,128]{1,0:T(8,128)S(1)} %add.16), channel_id=1, source_target_pairs={{0,5},{1,4},{2,7},{3,6},{4,1},{5,0},{6,3},{7,2},{8,13},{9,12},{10,... | collective-permute-start | bytes 147464 | tf_op jit(solution)/shard_map/ppermute | solution.py:590
  42.9 2.3 %collective-permute-done.8 = f32[96,128]{1,0:T(8,128)S(1)} collective-permute-done((f32[96,128]{1,0:T(8,128)S(1)}, f32[96,128]{1,0:T(8,128)S(1)}, u32[]{:S(2)}, u32[]{:S(2)}) %collective-permute-start.8) | collective-permute-done | bytes 49184 | tf_op jit(solution)/shard_map/ppermute | solution.py:590
  45.3 1.1 %collective-permute-start.9 = (f32[96,128]{1,0:T(8,128)S(1)}, f32[96,128]{1,0:T(8,128)S(1)}, u32[]{:S(2)}, u32[]{:S(2)}) collective-permute-start(f32[96,128]{1,0:T(8,128)S(1)} %add.17), channel_id=1, source_target_pairs={{0,9},{1,8},{2,11},{3,10},{4,13},{5,12},{6,15},{7,14},{8,1},{9,0},... | collective-permute-start | bytes 147464 | tf_op jit(solution)/shard_map/ppermute | solution.py:590
  46.3 2.7 %collective-permute-done.9 = f32[96,128]{1,0:T(8,128)S(1)} collective-permute-done((f32[96,128]{1,0:T(8,128)S(1)}, f32[96,128]{1,0:T(8,128)S(1)}, u32[]{:S(2)}, u32[]{:S(2)}) %collective-permute-start.9) | collective-permute-done | bytes 49184 | tf_op jit(solution)/shard_map/ppermute | solution.py:590
  49.1 0.6 collective-permute-start.10
  49.6 3.2 %collective-permute-done.10 = f32[96,128]{1,0:T(8,128)S(1)} collective-permute-done((f32[96,128]{1,0:T(8,128)S(1)}, f32[96,128]{1,0:T(8,128)S(1)}, u32[]{:S(2)}, u32[]{:S(2)}) %collective-permute-start.10) | collective-permute-done | bytes 49184 | tf_op jit(solution)/shard_map/ppermute | solution.py:590
  52.9 7.1 %shard_map.47 = (f32[96,64,128]{2,1,0:T(8,128)}, f32[96,96]{1,0:T(8,128)}) custom-call(f32[96,128]{1,0:T(8,128)S(1)} %add.19.sums_ref, f32[64,96,128]{2,1,0:T(8,128)S(1)} %get-tuple-element.59.turned), custom_call_target="tpu_custom_call" | custom-call | tf_op jit(solution)/shard_map/pallas_call | solution.py:549
  (5 shorter events, 0.0 us)
Async XLA Ops:
  4.5 14.0 %collective-permute-start.2 = (f32[864,128]{1,0:T(8,128)S(1)}, f32[864,128]{1,0:T(8,128)S(1)}, u32[]{:S(2)}, u32[]{:S(2)}) collective-permute-start(f32[864,128]{1,0:T(8,128)S(1)} %get-tuple-element.42), channel_id=1, source_target_pairs={{0,8},{8,0},{16,24},{24,16},{1,9},{9,1},{17,25},{25,17},{2,10},{10... | collective-permute-start | bytes 1327112 | tf_op jit(solution)/shard_map/ppermute | solution.py:601
  7.5 5.9 %collective-permute-start = (f32[576,128]{1,0:T(8,128)S(1)}, f32[576,128]{1,0:T(8,128)S(1)}, u32[]{:S(2)}, u32[]{:S(2)}) collective-permute-start(f32[576,128]{1,0:T(8,128)S(1)} %get-tuple-element.35), channel_id=1, source_target_pairs={{0,1},{1,0},{2,3},{3,2},{4,5},{5,4},{6,7},{7,6},{8,9},{9,8},{10,11... | collective-permute-start | bytes 884744 | tf_op jit(solution)/shard_map/ppermute | solution.py:599
  7.5 6.7 %collective-permute-start.1 = (f32[576,128]{1,0:T(8,128)S(1)}, f32[576,128]{1,0:T(8,128)S(1)}, u32[]{:S(2)}, u32[]{:S(2)}) collective-permute-start(f32[576,128]{1,0:T(8,128)S(1)} %get-tuple-element.36), channel_id=1, source_target_pairs={{0,16},{1,2},{2,1},{3,4},{4,3},{5,6},{6,5},{7,23},{8,24},{9,10},{1... | collective-permute-start | bytes 884744 | tf_op jit(solution)/shard_map/ppermute | solution.py:600
  9.1 21.7 %collective-permute-start.4 = (f32[480,128]{1,0:T(8,128)S(1)}, f32[480,128]{1,0:T(8,128)S(1)}, u32[]{:S(2)}, u32[]{:S(2)}) collective-permute-start(f32[480,128]{1,0:T(8,128)S(1)} %get-tuple-element.56), channel_id=1, source_target_pairs={{8,16},{16,8},{24,0},{0,24},{9,17},{17,9},{25,1},{1,25},{10,18},{1... | collective-permute-start | bytes 737288 | tf_op jit(solution)/shard_map/ppermute | solution.py:602
  15.1 12.9 %collective-permute-start.3 = (f32[160,128]{1,0:T(8,128)S(1)}, f32[160,128]{1,0:T(8,128)S(1)}, u32[]{:S(2)}, u32[]{:S(2)}) collective-permute-start(f32[160,128]{1,0:T(8,128)S(1)} %get-tuple-element.49), channel_id=1, source_target_pairs={{0,8},{8,0},{16,24},{24,16},{1,9},{9,1},{17,25},{25,17},{2,10},{10... | collective-permute-start | bytes 245768 | tf_op jit(solution)/shard_map/ppermute | solution.py:605
  16.2 15.7 %collective-permute-start.5 = (f32[544,128]{1,0:T(8,128)S(1)}, f32[544,128]{1,0:T(8,128)S(1)}, u32[]{:S(2)}, u32[]{:S(2)}) collective-permute-start(f32[544,128]{1,0:T(8,128)S(1)} %get-tuple-element.57), channel_id=1, source_target_pairs={{8,16},{16,8},{24,0},{0,24},{9,17},{17,9},{25,1},{1,25},{10,18},{1... | collective-permute-start | bytes 835592 | tf_op jit(solution)/shard_map/ppermute | solution.py:606
  35.4 1.3 %collective-permute-start.6 = (f32[96,128]{1,0:T(8,128)S(1)}, f32[96,128]{1,0:T(8,128)S(1)}, u32[]{:S(2)}, u32[]{:S(2)}) collective-permute-start(f32[96,128]{1,0:T(8,128)S(1)} %get-tuple-element.58), channel_id=1, source_target_pairs={{0,1},{1,0},{2,3},{3,2},{4,5},{5,4},{6,7},{7,6},{8,9},{9,8},{10,11... | collective-permute-start | bytes 147464 | tf_op jit(solution)/shard_map/ppermute | solution.py:590
  36.7 3.8 %collective-permute-start.7 = (f32[96,128]{1,0:T(8,128)S(1)}, f32[96,128]{1,0:T(8,128)S(1)}, u32[]{:S(2)}, u32[]{:S(2)}) collective-permute-start(f32[96,128]{1,0:T(8,128)S(1)} %add.15), channel_id=1, source_target_pairs={{0,3},{1,2},{2,1},{3,0},{4,7},{5,6},{6,5},{7,4},{8,11},{9,10},{10,... | collective-permute-start | bytes 147464 | tf_op jit(solution)/shard_map/ppermute | solution.py:590
  40.6 4.7 %collective-permute-start.8 = (f32[96,128]{1,0:T(8,128)S(1)}, f32[96,128]{1,0:T(8,128)S(1)}, u32[]{:S(2)}, u32[]{:S(2)}) collective-permute-start(f32[96,128]{1,0:T(8,128)S(1)} %add.16), channel_id=1, source_target_pairs={{0,5},{1,4},{2,7},{3,6},{4,1},{5,0},{6,3},{7,2},{8,13},{9,12},{10,... | collective-permute-start | bytes 147464 | tf_op jit(solution)/shard_map/ppermute | solution.py:590
  45.3 3.8 %collective-permute-start.9 = (f32[96,128]{1,0:T(8,128)S(1)}, f32[96,128]{1,0:T(8,128)S(1)}, u32[]{:S(2)}, u32[]{:S(2)}) collective-permute-start(f32[96,128]{1,0:T(8,128)S(1)} %add.17), channel_id=1, source_target_pairs={{0,9},{1,8},{2,11},{3,10},{4,13},{5,12},{6,15},{7,14},{8,1},{9,0},... | collective-permute-start | bytes 147464 | tf_op jit(solution)/shard_map/ppermute | solution.py:590
  49.1 3.8 %collective-permute-start.10 = (f32[96,128]{1,0:T(8,128)S(1)}, f32[96,128]{1,0:T(8,128)S(1)}, u32[]{:S(2)}, u32[]{:S(2)}) collective-permute-start(f32[96,128]{1,0:T(8,128)S(1)} %add.18), channel_id=1, source_target_pairs={{0,17},{1,16},{2,19},{3,18},{4,21},{5,20},{6,23},{7,22},{8,25},{9,... | collective-permute-start | bytes 147464 | tf_op jit(solution)/shard_map/ppermute | solution.py:590

commit v3 on v2

--- a/solution.py
+++ b/solution.py
@@ -90,7 +90,9 @@
         copies[i].wait()
         for r in range(step):
             x = i * step + r
-            turned = lanes_up(held[i, :, r, :], stiff[x : x + 1, :])
+            if r % 8 == 0:
+                eight = jnp.swapaxes(held[i, :, r : r + 8, :], 0, 1)
+            turned = lanes_up(eight[r % 8], stiff[x : x + 1, :])
             field[HALO + x, PAD : PAD + cols, :] = turned
             head, tail = turned[:HALO], turned[cols - HALO :]
             near[x * HALO : (x + 1) * HALO, :] = jnp.where(col_first, tail, head)
@@ -263,7 +265,7 @@
 
 def early_kernel(field_in, stiff_ref, field, stiff, odd, inner):
     rows, cols = stiff_ref.shape
-    step = 8
+    step = 32
 
     def some(i):
         for r in range(step):
@@ -514,14 +516,15 @@
     group = 8
     copies = []
     for x in range(0, rows, group):
+        found = []
         for g in range(0, group, 2):
             pair = jnp.concatenate([turned[x + g], turned[x + g + 1]], axis=1)
             pair_high, pair_low = split(pair)
             result = jnp.dot(high, pair_low, preferred_element_type=F32)
             result += jnp.dot(low, pair_high, preferred_element_type=F32)
             result += jnp.dot(high, pair_high, preferred_element_type=F32)
-            basis[:, x + g, :] = result[:, :cols]
-            basis[:, x + g + 1, :] = result[:, cols:]
+            found += [result[:, :cols], result[:, cols:]]
+        basis[:, x : x + group, :] = jnp.swapaxes(jnp.stack(found), 0, 1)
         copies.append(
             pltpu.make_async_copy(
                 basis.at[:, pl.ds(x, group), :], basis_ref.at[:, pl.ds(x, group), :], out_sems.at[x // group]

time: 60.4 us -> 58.9 us (0.975)
  Pallas kernels: 31.8 us -> 30 us
    pallas_call x1, Pallas kernels: 7.11 us -> 6.33 us  [finish(): pl.pallas_call(functools.partial(finish_kernel, scale), in_specs=[VMEM, V...]
    pallas_call x1, Pallas kernels: 3.89 us -> 3.26 us  [turn(): pl.pallas_call(turn_kernel, in_specs=[HBM] * 2, out_specs=[VMEM] * 7, out...]
where the time goes in v3:
time: 58.9 us; the launch traced here: 58.7 us
  Pallas kernels  30 us (51%)
  waiting for transfers between devices  14.8 us (25%)
  starting transfers between devices  13.1 us (22%)
  between operations  0.87 us (1%)
    ppermute x5, waiting for transfers between devices, all_sum(): lax.ppermute(values, axes, [(i, i ^ (step | 1)) for i in range(count)])  12 us
    pallas_call x1, Pallas kernels, middle(): pl.pallas_call(functools.partial(middle_kernel, vectors, rows, cols), in_...  9.41 us
    pallas_call x2, Pallas kernels, end(): pl.pallas_call(functools.partial(end_kernel, vectors, rows, cols, last),...  6.36 us
    pallas_call x1, Pallas kernels, finish(): pl.pallas_call(functools.partial(finish_kernel, scale), in_specs=[VMEM, V...  6.33 us
    ppermute x5, starting transfers between devices, all_sum(): lax.ppermute(values, axes, [(i, i ^ (step | 1)) for i in range(count)])  5.41 us
    pallas_call x1, Pallas kernels, early(): pl.pallas_call(early_kernel, in_specs=[VMEM] * 2, out_specs=[VMEM] * 4, o...  3.83 us
    pallas_call x1, Pallas kernels, turn(): pl.pallas_call(turn_kernel, in_specs=[HBM] * 2, out_specs=[VMEM] * 7, out...  3.26 us
    ppermute x1, starting transfers between devices, body(): one = lax.ppermute(one, 'row', pairs(row_count, 0))  3 us
  transfers between devices with their start and end apart: 11, of which 8 were waited for; matrix products, arithmetic and copies ran while one was open for 0% of the time, Pallas kernels for 29%

profile of v3, /device:TPU:0, one launch (start us, length us, event | category | flops | bytes accessed | tf_op | source)
XLA Modules:
  0.0 58.7 jit_solution(15983495224257425237)
XLA Ops:
  0.6 3.3 %shard_map.41 = (f32[82,160,128]{2,1,0:T(8,128)S(1)}, f32[576,128]{1,0:T(8,128)S(1)}, f32[576,128]{1,0:T(8,128)S(1)}, f32[864,128]{1,0:T(8,128)S(1)}, f32[480,12...) custom-call(f32[96,64,128]{2,1,0:T(8,128)} %block_ref.1, f32[64,128]{1,0:T(8,128)} %stiff_ref.1), custom_call_target="tpu_custom_call" | custom-call | bytes 6291456 | tf_op jit(solution)/shard_map/pallas_call | solution.py:112
  3.9 3.0 %collective-permute-start.2 = (f32[864,128]{1,0:T(8,128)S(1)}, f32[864,128]{1,0:T(8,128)S(1)}, u32[]{:S(2)}, u32[]{:S(2)}) collective-permute-start(f32[864,128]{1,0:T(8,128)S(1)} %get-tuple-element.42), channel_id=1, source_target_pairs={{0,8},{8,0},{16,24},{24,16},{1,9},{9,1},{17,25},{25,17},{2,10},{10... | collective-permute-start | bytes 1327112 | tf_op jit(solution)/shard_map/ppermute | solution.py:604
  6.9 0.0 collective-permute-start
  6.9 1.5 %collective-permute-start.1 = (f32[576,128]{1,0:T(8,128)S(1)}, f32[576,128]{1,0:T(8,128)S(1)}, u32[]{:S(2)}, u32[]{:S(2)}) collective-permute-start(f32[576,128]{1,0:T(8,128)S(1)} %get-tuple-element.36), channel_id=1, source_target_pairs={{0,16},{1,2},{2,1},{3,4},{4,3},{5,6},{6,5},{7,23},{8,24},{9,10},{1... | collective-permute-start | bytes 884744 | tf_op jit(solution)/shard_map/ppermute | solution.py:603
  8.4 0.1 collective-permute-start.4
  8.5 3.8 %shard_map.42 = (f32[82,160,128]{2,1,0:T(8,128)S(1)}, f32[82,160,128]{2,1,0:T(8,128)S(1)}, f32[82,160,128]{2,1,0:T(8,128)S(1)}, f32[82,160,128]{2,1,0:T(8,128)S(1)}) custom-call(f32[82,160,128]{2,1,0:T(8,128)S(1)} %get-tuple-element.31.field_in, f32[64,128]{1,0:T(8,128)S(1)} %get-tuple-element.32.stiff_ref), custom_call_target="tpu_custom_call", output_to_operand_aliasing={{0}: (0, {})} | custom-call | tf_op jit(solution)/shard_map/pallas_call | solution.py:283
  12.4 0.0 collective-permute-done.near
  12.4 1.3 %collective-permute-done.1.far = f32[576,128]{1,0:T(8,128)S(1)} collective-permute-done((f32[576,128]{1,0:T(8,128)S(1)}, f32[576,128]{1,0:T(8,128)S(1)}, u32[]{:S(2)}, u32[]{:S(2)}) %collective-permute-start.1) | collective-permute-done | bytes 294944 | tf_op jit(solution)/shard_map/ppermute | solution.py:603
  13.6 0.8 %shard_map.43 = (f32[82,160,128]{2,1,0:T(8,128)S(1)}, f32[82,160,128]{2,1,0:T(8,128)S(1)}, f32[160,128]{1,0:T(8,128)S(1)}, f32[544,128]{1,0:T(8,128)S(1)}) custom-call(f32[82,160,128]{2,1,0:T(8,128)S(1)} %get-tuple-element.33.field_in, f32[82,160,128]{2,1,0:T(8,128)S(1)} %get-tuple-element.34.stiff_in, ...), custom_call_target="tpu_custom_call", output_to_operand_aliasing={{0}: (0, {}), {1}: (1, {})} | custom-call | tf_op jit(solution)/shard_map/pallas_call | solution.py:179
  14.4 0.7 %collective-permute-start.3 = (f32[160,128]{1,0:T(8,128)S(1)}, f32[160,128]{1,0:T(8,128)S(1)}, u32[]{:S(2)}, u32[]{:S(2)}) collective-permute-start(f32[160,128]{1,0:T(8,128)S(1)} %get-tuple-element.49), channel_id=1, source_target_pairs={{0,8},{8,0},{16,24},{24,16},{1,9},{9,1},{17,25},{25,17},{2,10},{10... | collective-permute-start | bytes 245768 | tf_op jit(solution)/shard_map/ppermute | solution.py:608
  15.1 2.3 %collective-permute-start.5 = (f32[544,128]{1,0:T(8,128)S(1)}, f32[544,128]{1,0:T(8,128)S(1)}, u32[]{:S(2)}, u32[]{:S(2)}) collective-permute-start(f32[544,128]{1,0:T(8,128)S(1)} %get-tuple-element.57), channel_id=1, source_target_pairs={{8,16},{16,8},{24,0},{0,24},{9,17},{17,9},{25,1},{1,25},{10,18},{1... | collective-permute-start | bytes 835592 | tf_op jit(solution)/shard_map/ppermute | solution.py:609
  17.5 0.4 collective-permute-done.2.one
  17.9 9.4 %shard_map.44 = (f32[82,160,128]{2,1,0:T(8,128)S(1)}, f32[82,160,128]{2,1,0:T(8,128)S(1)}, f32[82,160,128]{2,1,0:T(8,128)S(1)}, f32[82,160,128]{2,1,0:T(8,128)S(...) custom-call(f32[82,160,128]{2,1,0:T(8,128)S(1)} %get-tuple-element.3, ...), custom_call_target="tpu_custom_call", output_to_operand_aliasing={{0}: (0, {}), {1}: (1, {}), {2}: (2, {}), {3}: (3, {})} | custom-call | flops 10000000000 | bytes 41943040 | tf_op jit(solution)/shard_map/pallas_call | solution.py:354
  27.3 0.0 collective-permute-done.3.refs_0_
  27.3 2.8 %shard_map.45 = (f32[82,160,128]{2,1,0:T(8,128)S(1)}, f32[82,160,128]{2,1,0:T(8,128)S(1)}, f32[82,160,128]{2,1,0:T(8,128)S(1)}, f32[82,160,128]{2,1,0:T(8,128)S(...) custom-call(f32[82,160,128]{2,1,0:T(8,128)S(1)} %get-tuple-element.4, ...), custom_call_target="tpu_custom_call", output_to_operand_aliasing={{0}: (0, {}), {1}: (1, {}), {2}: (2, {}), {3}: (3, {}), {4}... | custom-call | tf_op jit(solution)/shard_map/pallas_call | solution.py:453
  30.2 0.0 collective-permute-done.4.refs_0_
  30.2 1.1 %collective-permute-done.5.refs_1_ = f32[544,128]{1,0:T(8,128)S(1)} collective-permute-done((f32[544,128]{1,0:T(8,128)S(1)}, f32[544,128]{1,0:T(8,128)S(1)}, u32[]{:S(2)}, u32[]{:S(2)}) %collective-permute-start.5) | collective-permute-done | bytes 278560 | tf_op jit(solution)/shard_map/ppermute | solution.py:609
  31.3 3.5 %shard_map.46 = (f32[82,160,128]{2,1,0:T(8,128)S(1)}, f32[82,160,128]{2,1,0:T(8,128)S(1)}, f32[82,160,128]{2,1,0:T(8,128)S(1)}, f32[82,160,128]{2,1,0:T(8,128)S(...) custom-call(f32[82,160,128]{2,1,0:T(8,128)S(1)} %get-tuple-element.5, ...), custom_call_target="tpu_custom_call", output_to_operand_aliasing={{0}: (0, {}), {1}: (1, {}), {2}: (2, {}), {3}: (3, {}), {4}... | custom-call | tf_op jit(solution)/shard_map/pallas_call | solution.py:453
  34.8 0.1 collective-permute-start.6
  34.9 1.2 %collective-permute-done.6 = f32[96,128]{1,0:T(8,128)S(1)} collective-permute-done((f32[96,128]{1,0:T(8,128)S(1)}, f32[96,128]{1,0:T(8,128)S(1)}, u32[]{:S(2)}, u32[]{:S(2)}) %collective-permute-start.6) | collective-permute-done | bytes 49184 | tf_op jit(solution)/shard_map/ppermute | solution.py:593
  36.1 1.3 %collective-permute-start.7 = (f32[96,128]{1,0:T(8,128)S(1)}, f32[96,128]{1,0:T(8,128)S(1)}, u32[]{:S(2)}, u32[]{:S(2)}) collective-permute-start(f32[96,128]{1,0:T(8,128)S(1)} %add.15), channel_id=1, source_target_pairs={{0,3},{1,2},{2,1},{3,0},{4,7},{5,6},{6,5},{7,4},{8,11},{9,10},{10,... | collective-permute-start | bytes 147464 | tf_op jit(solution)/shard_map/ppermute | solution.py:593
  37.4 2.5 %collective-permute-done.7 = f32[96,128]{1,0:T(8,128)S(1)} collective-permute-done((f32[96,128]{1,0:T(8,128)S(1)}, f32[96,128]{1,0:T(8,128)S(1)}, u32[]{:S(2)}, u32[]{:S(2)}) %collective-permute-start.7) | collective-permute-done | bytes 49184 | tf_op jit(solution)/shard_map/ppermute | solution.py:593
  39.9 2.4 %collective-permute-start.8 = (f32[96,128]{1,0:T(8,128)S(1)}, f32[96,128]{1,0:T(8,128)S(1)}, u32[]{:S(2)}, u32[]{:S(2)}) collective-permute-start(f32[96,128]{1,0:T(8,128)S(1)} %add.16), channel_id=1, source_target_pairs={{0,5},{1,4},{2,7},{3,6},{4,1},{5,0},{6,3},{7,2},{8,13},{9,12},{10,... | collective-permute-start | bytes 147464 | tf_op jit(solution)/shard_map/ppermute | solution.py:593
  42.3 2.3 %collective-permute-done.8 = f32[96,128]{1,0:T(8,128)S(1)} collective-permute-done((f32[96,128]{1,0:T(8,128)S(1)}, f32[96,128]{1,0:T(8,128)S(1)}, u32[]{:S(2)}, u32[]{:S(2)}) %collective-permute-start.8) | collective-permute-done | bytes 49184 | tf_op jit(solution)/shard_map/ppermute | solution.py:593
  44.6 1.1 %collective-permute-start.9 = (f32[96,128]{1,0:T(8,128)S(1)}, f32[96,128]{1,0:T(8,128)S(1)}, u32[]{:S(2)}, u32[]{:S(2)}) collective-permute-start(f32[96,128]{1,0:T(8,128)S(1)} %add.17), channel_id=1, source_target_pairs={{0,9},{1,8},{2,11},{3,10},{4,13},{5,12},{6,15},{7,14},{8,1},{9,0},... | collective-permute-start | bytes 147464 | tf_op jit(solution)/shard_map/ppermute | solution.py:593
  45.7 2.7 %collective-permute-done.9 = f32[96,128]{1,0:T(8,128)S(1)} collective-permute-done((f32[96,128]{1,0:T(8,128)S(1)}, f32[96,128]{1,0:T(8,128)S(1)}, u32[]{:S(2)}, u32[]{:S(2)}) %collective-permute-start.9) | collective-permute-done | bytes 49184 | tf_op jit(solution)/shard_map/ppermute | solution.py:593
  48.4 0.6 collective-permute-start.10
  49.0 3.2 %collective-permute-done.10 = f32[96,128]{1,0:T(8,128)S(1)} collective-permute-done((f32[96,128]{1,0:T(8,128)S(1)}, f32[96,128]{1,0:T(8,128)S(1)}, u32[]{:S(2)}, u32[]{:S(2)}) %collective-permute-start.10) | collective-permute-done | bytes 49184 | tf_op jit(solution)/shard_map/ppermute | solution.py:593
  52.2 6.3 %shard_map.47 = (f32[96,64,128]{2,1,0:T(8,128)}, f32[96,96]{1,0:T(8,128)}) custom-call(f32[96,128]{1,0:T(8,128)S(1)} %add.19.sums_ref, f32[64,96,128]{2,1,0:T(8,128)S(1)} %get-tuple-element.59.turned), custom_call_target="tpu_custom_call" | custom-call | tf_op jit(solution)/shard_map/pallas_call | solution.py:552
  (5 shorter events, 0.0 us)
Async XLA Ops:
  3.9 14.0 %collective-permute-start.2 = (f32[864,128]{1,0:T(8,128)S(1)}, f32[864,128]{1,0:T(8,128)S(1)}, u32[]{:S(2)}, u32[]{:S(2)}) collective-permute-start(f32[864,128]{1,0:T(8,128)S(1)} %get-tuple-element.42), channel_id=1, source_target_pairs={{0,8},{8,0},{16,24},{24,16},{1,9},{9,1},{17,25},{25,17},{2,10},{10... | collective-permute-start | bytes 1327112 | tf_op jit(solution)/shard_map/ppermute | solution.py:604
  6.9 5.5 %collective-permute-start = (f32[576,128]{1,0:T(8,128)S(1)}, f32[576,128]{1,0:T(8,128)S(1)}, u32[]{:S(2)}, u32[]{:S(2)}) collective-permute-start(f32[576,128]{1,0:T(8,128)S(1)} %get-tuple-element.35), channel_id=1, source_target_pairs={{0,1},{1,0},{2,3},{3,2},{4,5},{5,4},{6,7},{7,6},{8,9},{9,8},{10,11... | collective-permute-start | bytes 884744 | tf_op jit(solution)/shard_map/ppermute | solution.py:602
  6.9 6.7 %collective-permute-start.1 = (f32[576,128]{1,0:T(8,128)S(1)}, f32[576,128]{1,0:T(8,128)S(1)}, u32[]{:S(2)}, u32[]{:S(2)}) collective-permute-start(f32[576,128]{1,0:T(8,128)S(1)} %get-tuple-element.36), channel_id=1, source_target_pairs={{0,16},{1,2},{2,1},{3,4},{4,3},{5,6},{6,5},{7,23},{8,24},{9,10},{1... | collective-permute-start | bytes 884744 | tf_op jit(solution)/shard_map/ppermute | solution.py:603
  8.4 21.7 %collective-permute-start.4 = (f32[480,128]{1,0:T(8,128)S(1)}, f32[480,128]{1,0:T(8,128)S(1)}, u32[]{:S(2)}, u32[]{:S(2)}) collective-permute-start(f32[480,128]{1,0:T(8,128)S(1)} %get-tuple-element.56), channel_id=1, source_target_pairs={{8,16},{16,8},{24,0},{0,24},{9,17},{17,9},{25,1},{1,25},{10,18},{1... | collective-permute-start | bytes 737288 | tf_op jit(solution)/shard_map/ppermute | solution.py:605
  14.4 12.9 %collective-permute-start.3 = (f32[160,128]{1,0:T(8,128)S(1)}, f32[160,128]{1,0:T(8,128)S(1)}, u32[]{:S(2)}, u32[]{:S(2)}) collective-permute-start(f32[160,128]{1,0:T(8,128)S(1)} %get-tuple-element.49), channel_id=1, source_target_pairs={{0,8},{8,0},{16,24},{24,16},{1,9},{9,1},{17,25},{25,17},{2,10},{10... | collective-permute-start | bytes 245768 | tf_op jit(solution)/shard_map/ppermute | solution.py:608
  15.1 16.1 %collective-permute-start.5 = (f32[544,128]{1,0:T(8,128)S(1)}, f32[544,128]{1,0:T(8,128)S(1)}, u32[]{:S(2)}, u32[]{:S(2)}) collective-permute-start(f32[544,128]{1,0:T(8,128)S(1)} %get-tuple-element.57), channel_id=1, source_target_pairs={{8,16},{16,8},{24,0},{0,24},{9,17},{17,9},{25,1},{1,25},{10,18},{1... | collective-permute-start | bytes 835592 | tf_op jit(solution)/shard_map/ppermute | solution.py:609
  34.8 1.3 %collective-permute-start.6 = (f32[96,128]{1,0:T(8,128)S(1)}, f32[96,128]{1,0:T(8,128)S(1)}, u32[]{:S(2)}, u32[]{:S(2)}) collective-permute-start(f32[96,128]{1,0:T(8,128)S(1)} %get-tuple-element.58), channel_id=1, source_target_pairs={{0,1},{1,0},{2,3},{3,2},{4,5},{5,4},{6,7},{7,6},{8,9},{9,8},{10,11... | collective-permute-start | bytes 147464 | tf_op jit(solution)/shard_map/ppermute | solution.py:593
  36.1 3.8 %collective-permute-start.7 = (f32[96,128]{1,0:T(8,128)S(1)}, f32[96,128]{1,0:T(8,128)S(1)}, u32[]{:S(2)}, u32[]{:S(2)}) collective-permute-start(f32[96,128]{1,0:T(8,128)S(1)} %add.15), channel_id=1, source_target_pairs={{0,3},{1,2},{2,1},{3,0},{4,7},{5,6},{6,5},{7,4},{8,11},{9,10},{10,... | collective-permute-start | bytes 147464 | tf_op jit(solution)/shard_map/ppermute | solution.py:593
  39.9 4.7 %collective-permute-start.8 = (f32[96,128]{1,0:T(8,128)S(1)}, f32[96,128]{1,0:T(8,128)S(1)}, u32[]{:S(2)}, u32[]{:S(2)}) collective-permute-start(f32[96,128]{1,0:T(8,128)S(1)} %add.16), channel_id=1, source_target_pairs={{0,5},{1,4},{2,7},{3,6},{4,1},{5,0},{6,3},{7,2},{8,13},{9,12},{10,... | collective-permute-start | bytes 147464 | tf_op jit(solution)/shard_map/ppermute | solution.py:593
  44.6 3.8 %collective-permute-start.9 = (f32[96,128]{1,0:T(8,128)S(1)}, f32[96,128]{1,0:T(8,128)S(1)}, u32[]{:S(2)}, u32[]{:S(2)}) collective-permute-start(f32[96,128]{1,0:T(8,128)S(1)} %add.17), channel_id=1, source_target_pairs={{0,9},{1,8},{2,11},{3,10},{4,13},{5,12},{6,15},{7,14},{8,1},{9,0},... | collective-permute-start | bytes 147464 | tf_op jit(solution)/shard_map/ppermute | solution.py:593
  48.4 3.8 %collective-permute-start.10 = (f32[96,128]{1,0:T(8,128)S(1)}, f32[96,128]{1,0:T(8,128)S(1)}, u32[]{:S(2)}, u32[]{:S(2)}) collective-permute-start(f32[96,128]{1,0:T(8,128)S(1)} %add.18), channel_id=1, source_target_pairs={{0,17},{1,16},{2,19},{3,18},{4,21},{5,20},{6,23},{7,22},{8,25},{9,... | collective-permute-start | bytes 147464 | tf_op jit(solution)/shard_map/ppermute | solution.py:593

commit v4 on v3

--- a/solution.py
+++ b/solution.py
@@ -16,7 +16,7 @@
 HALO = 2 * DEGREE + 1
 MARGIN = HALO - 1
 FIRST = 5
-EARLY = 2
+EARLY = 3
 LANES = 128
 PAD = 16
 GROUP = 4

time: 58.9 us -> 58.9 us (level)
  no operation moved by 1% of the time
where the time goes in v4:
time: 58.9 us; the launch traced here: 58.7 us
  Pallas kernels  30.1 us (51%)
  waiting for transfers between devices  15.1 us (26%)
  starting transfers between devices  12.6 us (21%)
  between operations  0.87 us (1%)
    ppermute x5, waiting for transfers between devices, all_sum(): lax.ppermute(values, axes, [(i, i ^ (step | 1)) for i in range(count)])  12.4 us
    pallas_call x1, Pallas kernels, middle(): pl.pallas_call(functools.partial(middle_kernel, vectors, rows, cols), in_...  8.95 us
    pallas_call x2, Pallas kernels, end(): pl.pallas_call(functools.partial(end_kernel, vectors, rows, cols, last),...  6.36 us
    pallas_call x1, Pallas kernels, finish(): pl.pallas_call(functools.partial(finish_kernel, scale), in_specs=[VMEM, V...  6.33 us
    ppermute x5, starting transfers between devices, all_sum(): lax.ppermute(values, axes, [(i, i ^ (step | 1)) for i in range(count)])  4.95 us
    pallas_call x1, Pallas kernels, early(): pl.pallas_call(early_kernel, in_specs=[VMEM] * 2, out_specs=[VMEM] * 4, o...  4.39 us
    pallas_call x1, Pallas kernels, turn(): pl.pallas_call(turn_kernel, in_specs=[HBM] * 2, out_specs=[VMEM] * 7, out...  3.26 us
    ppermute x1, starting transfers between devices, body(): one = lax.ppermute(one, 'row', pairs(row_count, 0))  3 us
  transfers between devices with their start and end apart: 11, of which 8 were waited for; matrix products, arithmetic and copies ran while one was open for 0% of the time, Pallas kernels for 29%

profile of v4, /device:TPU:0, one launch (start us, length us, event | category | flops | bytes accessed | tf_op | source)
XLA Modules:
  0.0 58.7 jit_solution(13266280862525086181)
XLA Ops:
  0.6 3.3 %shard_map.41 = (f32[82,160,128]{2,1,0:T(8,128)S(1)}, f32[576,128]{1,0:T(8,128)S(1)}, f32[576,128]{1,0:T(8,128)S(1)}, f32[864,128]{1,0:T(8,128)S(1)}, f32[480,12...) custom-call(f32[96,64,128]{2,1,0:T(8,128)} %block_ref.1, f32[64,128]{1,0:T(8,128)} %stiff_ref.1), custom_call_target="tpu_custom_call" | custom-call | bytes 6291456 | tf_op jit(solution)/shard_map/pallas_call | solution.py:112
  3.9 3.0 %collective-permute-start.2 = (f32[864,128]{1,0:T(8,128)S(1)}, f32[864,128]{1,0:T(8,128)S(1)}, u32[]{:S(2)}, u32[]{:S(2)}) collective-permute-start(f32[864,128]{1,0:T(8,128)S(1)} %get-tuple-element.42), channel_id=1, source_target_pairs={{0,8},{8,0},{16,24},{24,16},{1,9},{9,1},{17,25},{25,17},{2,10},{10... | collective-permute-start | bytes 1327112 | tf_op jit(solution)/shard_map/ppermute | solution.py:604
  6.9 0.0 collective-permute-start
  6.9 1.5 %collective-permute-start.1 = (f32[576,128]{1,0:T(8,128)S(1)}, f32[576,128]{1,0:T(8,128)S(1)}, u32[]{:S(2)}, u32[]{:S(2)}) collective-permute-start(f32[576,128]{1,0:T(8,128)S(1)} %get-tuple-element.36), channel_id=1, source_target_pairs={{0,16},{1,2},{2,1},{3,4},{4,3},{5,6},{6,5},{7,23},{8,24},{9,10},{1... | collective-permute-start | bytes 884744 | tf_op jit(solution)/shard_map/ppermute | solution.py:603
  8.4 0.1 collective-permute-start.4
  8.5 4.4 %shard_map.42 = (f32[82,160,128]{2,1,0:T(8,128)S(1)}, f32[82,160,128]{2,1,0:T(8,128)S(1)}, f32[82,160,128]{2,1,0:T(8,128)S(1)}, f32[82,160,128]{2,1,0:T(8,128)S(1)}) custom-call(f32[82,160,128]{2,1,0:T(8,128)S(1)} %get-tuple-element.31.field_in, f32[64,128]{1,0:T(8,128)S(1)} %get-tuple-element.32.stiff_ref), custom_call_target="tpu_custom_call", output_to_operand_aliasing={{0}: (0, {})} | custom-call | tf_op jit(solution)/shard_map/pallas_call | solution.py:283
  12.9 0.0 collective-permute-done.near
  12.9 0.7 %collective-permute-done.1.far = f32[576,128]{1,0:T(8,128)S(1)} collective-permute-done((f32[576,128]{1,0:T(8,128)S(1)}, f32[576,128]{1,0:T(8,128)S(1)}, u32[]{:S(2)}, u32[]{:S(2)}) %collective-permute-start.1) | collective-permute-done | bytes 294944 | tf_op jit(solution)/shard_map/ppermute | solution.py:603
  13.6 0.8 %shard_map.43 = (f32[82,160,128]{2,1,0:T(8,128)S(1)}, f32[82,160,128]{2,1,0:T(8,128)S(1)}, f32[160,128]{1,0:T(8,128)S(1)}, f32[544,128]{1,0:T(8,128)S(1)}) custom-call(f32[82,160,128]{2,1,0:T(8,128)S(1)} %get-tuple-element.33.field_in, f32[82,160,128]{2,1,0:T(8,128)S(1)} %get-tuple-element.34.stiff_in, ...), custom_call_target="tpu_custom_call", output_to_operand_aliasing={{0}: (0, {}), {1}: (1, {})} | custom-call | tf_op jit(solution)/shard_map/pallas_call | solution.py:179
  14.4 1.3 %collective-permute-start.3 = (f32[160,128]{1,0:T(8,128)S(1)}, f32[160,128]{1,0:T(8,128)S(1)}, u32[]{:S(2)}, u32[]{:S(2)}) collective-permute-start(f32[160,128]{1,0:T(8,128)S(1)} %get-tuple-element.49), channel_id=1, source_target_pairs={{0,8},{8,0},{16,24},{24,16},{1,9},{9,1},{17,25},{25,17},{2,10},{10... | collective-permute-start | bytes 245768 | tf_op jit(solution)/shard_map/ppermute | solution.py:608
  15.7 1.8 %collective-permute-start.5 = (f32[544,128]{1,0:T(8,128)S(1)}, f32[544,128]{1,0:T(8,128)S(1)}, u32[]{:S(2)}, u32[]{:S(2)}) collective-permute-start(f32[544,128]{1,0:T(8,128)S(1)} %get-tuple-element.57), channel_id=1, source_target_pairs={{8,16},{16,8},{24,0},{0,24},{9,17},{17,9},{25,1},{1,25},{10,18},{1... | collective-permute-start | bytes 835592 | tf_op jit(solution)/shard_map/ppermute | solution.py:609
  17.5 0.4 collective-permute-done.2.one
  17.9 8.9 %shard_map.44 = (f32[82,160,128]{2,1,0:T(8,128)S(1)}, f32[82,160,128]{2,1,0:T(8,128)S(1)}, f32[82,160,128]{2,1,0:T(8,128)S(1)}, f32[82,160,128]{2,1,0:T(8,128)S(...) custom-call(f32[82,160,128]{2,1,0:T(8,128)S(1)} %get-tuple-element.3, ...), custom_call_target="tpu_custom_call", output_to_operand_aliasing={{0}: (0, {}), {1}: (1, {}), {2}: (2, {}), {3}: (3, {})} | custom-call | flops 10000000000 | bytes 41943040 | tf_op jit(solution)/shard_map/pallas_call | solution.py:354
  26.8 0.0 collective-permute-done.3.refs_0_
  26.9 2.8 %shard_map.45 = (f32[82,160,128]{2,1,0:T(8,128)S(1)}, f32[82,160,128]{2,1,0:T(8,128)S(1)}, f32[82,160,128]{2,1,0:T(8,128)S(1)}, f32[82,160,128]{2,1,0:T(8,128)S(...) custom-call(f32[82,160,128]{2,1,0:T(8,128)S(1)} %get-tuple-element.4, ...), custom_call_target="tpu_custom_call", output_to_operand_aliasing={{0}: (0, {}), {1}: (1, {}), {2}: (2, {}), {3}: (3, {}), {4}... | custom-call | tf_op jit(solution)/shard_map/pallas_call | solution.py:453
  29.7 0.0 collective-permute-done.4.refs_0_
  29.7 1.6 %collective-permute-done.5.refs_1_ = f32[544,128]{1,0:T(8,128)S(1)} collective-permute-done((f32[544,128]{1,0:T(8,128)S(1)}, f32[544,128]{1,0:T(8,128)S(1)}, u32[]{:S(2)}, u32[]{:S(2)}) %collective-permute-start.5) | collective-permute-done | bytes 278560 | tf_op jit(solution)/shard_map/ppermute | solution.py:609
  31.3 3.5 %shard_map.46 = (f32[82,160,128]{2,1,0:T(8,128)S(1)}, f32[82,160,128]{2,1,0:T(8,128)S(1)}, f32[82,160,128]{2,1,0:T(8,128)S(1)}, f32[82,160,128]{2,1,0:T(8,128)S(...) custom-call(f32[82,160,128]{2,1,0:T(8,128)S(1)} %get-tuple-element.5, ...), custom_call_target="tpu_custom_call", output_to_operand_aliasing={{0}: (0, {}), {1}: (1, {}), {2}: (2, {}), {3}: (3, {}), {4}... | custom-call | tf_op jit(solution)/shard_map/pallas_call | solution.py:453
  34.8 0.1 collective-permute-start.6
  34.9 1.2 %collective-permute-done.6 = f32[96,128]{1,0:T(8,128)S(1)} collective-permute-done((f32[96,128]{1,0:T(8,128)S(1)}, f32[96,128]{1,0:T(8,128)S(1)}, u32[]{:S(2)}, u32[]{:S(2)}) %collective-permute-start.6) | collective-permute-done | bytes 49184 | tf_op jit(solution)/shard_map/ppermute | solution.py:593
  36.1 1.3 %collective-permute-start.7 = (f32[96,128]{1,0:T(8,128)S(1)}, f32[96,128]{1,0:T(8,128)S(1)}, u32[]{:S(2)}, u32[]{:S(2)}) collective-permute-start(f32[96,128]{1,0:T(8,128)S(1)} %add.15), channel_id=1, source_target_pairs={{0,3},{1,2},{2,1},{3,0},{4,7},{5,6},{6,5},{7,4},{8,11},{9,10},{10,... | collective-permute-start | bytes 147464 | tf_op jit(solution)/shard_map/ppermute | solution.py:593
  37.4 2.5 %collective-permute-done.7 = f32[96,128]{1,0:T(8,128)S(1)} collective-permute-done((f32[96,128]{1,0:T(8,128)S(1)}, f32[96,128]{1,0:T(8,128)S(1)}, u32[]{:S(2)}, u32[]{:S(2)}) %collective-permute-start.7) | collective-permute-done | bytes 49184 | tf_op jit(solution)/shard_map/ppermute | solution.py:593
  39.9 2.4 %collective-permute-start.8 = (f32[96,128]{1,0:T(8,128)S(1)}, f32[96,128]{1,0:T(8,128)S(1)}, u32[]{:S(2)}, u32[]{:S(2)}) collective-permute-start(f32[96,128]{1,0:T(8,128)S(1)} %add.16), channel_id=1, source_target_pairs={{0,5},{1,4},{2,7},{3,6},{4,1},{5,0},{6,3},{7,2},{8,13},{9,12},{10,... | collective-permute-start | bytes 147464 | tf_op jit(solution)/shard_map/ppermute | solution.py:593
  42.3 2.3 %collective-permute-done.8 = f32[96,128]{1,0:T(8,128)S(1)} collective-permute-done((f32[96,128]{1,0:T(8,128)S(1)}, f32[96,128]{1,0:T(8,128)S(1)}, u32[]{:S(2)}, u32[]{:S(2)}) %collective-permute-start.8) | collective-permute-done | bytes 49184 | tf_op jit(solution)/shard_map/ppermute | solution.py:593
  44.6 1.1 %collective-permute-start.9 = (f32[96,128]{1,0:T(8,128)S(1)}, f32[96,128]{1,0:T(8,128)S(1)}, u32[]{:S(2)}, u32[]{:S(2)}) collective-permute-start(f32[96,128]{1,0:T(8,128)S(1)} %add.17), channel_id=1, source_target_pairs={{0,9},{1,8},{2,11},{3,10},{4,13},{5,12},{6,15},{7,14},{8,1},{9,0},... | collective-permute-start | bytes 147464 | tf_op jit(solution)/shard_map/ppermute | solution.py:593
  45.7 2.7 %collective-permute-done.9 = f32[96,128]{1,0:T(8,128)S(1)} collective-permute-done((f32[96,128]{1,0:T(8,128)S(1)}, f32[96,128]{1,0:T(8,128)S(1)}, u32[]{:S(2)}, u32[]{:S(2)}) %collective-permute-start.9) | collective-permute-done | bytes 49184 | tf_op jit(solution)/shard_map/ppermute | solution.py:593
  48.4 0.1 collective-permute-start.10
  48.5 3.7 %collective-permute-done.10 = f32[96,128]{1,0:T(8,128)S(1)} collective-permute-done((f32[96,128]{1,0:T(8,128)S(1)}, f32[96,128]{1,0:T(8,128)S(1)}, u32[]{:S(2)}, u32[]{:S(2)}) %collective-permute-start.10) | collective-permute-done | bytes 49184 | tf_op jit(solution)/shard_map/ppermute | solution.py:593
  52.2 6.3 %shard_map.47 = (f32[96,64,128]{2,1,0:T(8,128)}, f32[96,96]{1,0:T(8,128)}) custom-call(f32[96,128]{1,0:T(8,128)S(1)} %add.19.sums_ref, f32[64,96,128]{2,1,0:T(8,128)S(1)} %get-tuple-element.59.turned), custom_call_target="tpu_custom_call" | custom-call | tf_op jit(solution)/shard_map/pallas_call | solution.py:552
  (5 shorter events, 0.0 us)
Async XLA Ops:
  3.9 14.0 %collective-permute-start.2 = (f32[864,128]{1,0:T(8,128)S(1)}, f32[864,128]{1,0:T(8,128)S(1)}, u32[]{:S(2)}, u32[]{:S(2)}) collective-permute-start(f32[864,128]{1,0:T(8,128)S(1)} %get-tuple-element.42), channel_id=1, source_target_pairs={{0,8},{8,0},{16,24},{24,16},{1,9},{9,1},{17,25},{25,17},{2,10},{10... | collective-permute-start | bytes 1327112 | tf_op jit(solution)/shard_map/ppermute | solution.py:604
  6.9 6.0 %collective-permute-start = (f32[576,128]{1,0:T(8,128)S(1)}, f32[576,128]{1,0:T(8,128)S(1)}, u32[]{:S(2)}, u32[]{:S(2)}) collective-permute-start(f32[576,128]{1,0:T(8,128)S(1)} %get-tuple-element.35), channel_id=1, source_target_pairs={{0,1},{1,0},{2,3},{3,2},{4,5},{5,4},{6,7},{7,6},{8,9},{9,8},{10,11... | collective-permute-start | bytes 884744 | tf_op jit(solution)/shard_map/ppermute | solution.py:602
  6.9 6.7 %collective-permute-start.1 = (f32[576,128]{1,0:T(8,128)S(1)}, f32[576,128]{1,0:T(8,128)S(1)}, u32[]{:S(2)}, u32[]{:S(2)}) collective-permute-start(f32[576,128]{1,0:T(8,128)S(1)} %get-tuple-element.36), channel_id=1, source_target_pairs={{0,16},{1,2},{2,1},{3,4},{4,3},{5,6},{6,5},{7,23},{8,24},{9,10},{1... | collective-permute-start | bytes 884744 | tf_op jit(solution)/shard_map/ppermute | solution.py:603
  8.4 21.3 %collective-permute-start.4 = (f32[480,128]{1,0:T(8,128)S(1)}, f32[480,128]{1,0:T(8,128)S(1)}, u32[]{:S(2)}, u32[]{:S(2)}) collective-permute-start(f32[480,128]{1,0:T(8,128)S(1)} %get-tuple-element.56), channel_id=1, source_target_pairs={{8,16},{16,8},{24,0},{0,24},{9,17},{17,9},{25,1},{1,25},{10,18},{1... | collective-permute-start | bytes 737288 | tf_op jit(solution)/shard_map/ppermute | solution.py:605
  14.4 12.4 %collective-permute-start.3 = (f32[160,128]{1,0:T(8,128)S(1)}, f32[160,128]{1,0:T(8,128)S(1)}, u32[]{:S(2)}, u32[]{:S(2)}) collective-permute-start(f32[160,128]{1,0:T(8,128)S(1)} %get-tuple-element.49), channel_id=1, source_target_pairs={{0,8},{8,0},{16,24},{24,16},{1,9},{9,1},{17,25},{25,17},{2,10},{10... | collective-permute-start | bytes 245768 | tf_op jit(solution)/shard_map/ppermute | solution.py:608
  15.7 15.6 %collective-permute-start.5 = (f32[544,128]{1,0:T(8,128)S(1)}, f32[544,128]{1,0:T(8,128)S(1)}, u32[]{:S(2)}, u32[]{:S(2)}) collective-permute-start(f32[544,128]{1,0:T(8,128)S(1)} %get-tuple-element.57), channel_id=1, source_target_pairs={{8,16},{16,8},{24,0},{0,24},{9,17},{17,9},{25,1},{1,25},{10,18},{1... | collective-permute-start | bytes 835592 | tf_op jit(solution)/shard_map/ppermute | solution.py:609
  34.8 1.3 %collective-permute-start.6 = (f32[96,128]{1,0:T(8,128)S(1)}, f32[96,128]{1,0:T(8,128)S(1)}, u32[]{:S(2)}, u32[]{:S(2)}) collective-permute-start(f32[96,128]{1,0:T(8,128)S(1)} %get-tuple-element.58), channel_id=1, source_target_pairs={{0,1},{1,0},{2,3},{3,2},{4,5},{5,4},{6,7},{7,6},{8,9},{9,8},{10,11... | collective-permute-start | bytes 147464 | tf_op jit(solution)/shard_map/ppermute | solution.py:593
  36.1 3.8 %collective-permute-start.7 = (f32[96,128]{1,0:T(8,128)S(1)}, f32[96,128]{1,0:T(8,128)S(1)}, u32[]{:S(2)}, u32[]{:S(2)}) collective-permute-start(f32[96,128]{1,0:T(8,128)S(1)} %add.15), channel_id=1, source_target_pairs={{0,3},{1,2},{2,1},{3,0},{4,7},{5,6},{6,5},{7,4},{8,11},{9,10},{10,... | collective-permute-start | bytes 147464 | tf_op jit(solution)/shard_map/ppermute | solution.py:593
  39.9 4.7 %collective-permute-start.8 = (f32[96,128]{1,0:T(8,128)S(1)}, f32[96,128]{1,0:T(8,128)S(1)}, u32[]{:S(2)}, u32[]{:S(2)}) collective-permute-start(f32[96,128]{1,0:T(8,128)S(1)} %add.16), channel_id=1, source_target_pairs={{0,5},{1,4},{2,7},{3,6},{4,1},{5,0},{6,3},{7,2},{8,13},{9,12},{10,... | collective-permute-start | bytes 147464 | tf_op jit(solution)/shard_map/ppermute | solution.py:593
  44.6 3.8 %collective-permute-start.9 = (f32[96,128]{1,0:T(8,128)S(1)}, f32[96,128]{1,0:T(8,128)S(1)}, u32[]{:S(2)}, u32[]{:S(2)}) collective-permute-start(f32[96,128]{1,0:T(8,128)S(1)} %add.17), channel_id=1, source_target_pairs={{0,9},{1,8},{2,11},{3,10},{4,13},{5,12},{6,15},{7,14},{8,1},{9,0},... | collective-permute-start | bytes 147464 | tf_op jit(solution)/shard_map/ppermute | solution.py:593
  48.4 3.8 %collective-permute-start.10 = (f32[96,128]{1,0:T(8,128)S(1)}, f32[96,128]{1,0:T(8,128)S(1)}, u32[]{:S(2)}, u32[]{:S(2)}) collective-permute-start(f32[96,128]{1,0:T(8,128)S(1)} %add.18), channel_id=1, source_target_pairs={{0,17},{1,16},{2,19},{3,18},{4,21},{5,20},{6,23},{7,22},{8,25},{9,... | collective-permute-start | bytes 147464 | tf_op jit(solution)/shard_map/ppermute | solution.py:593
